TPU v7x, 32 devices: a whole 2x2x4 slice. The times are simulated.
32 devices in a mesh: group: 4 (over y, x), dp: 2 (over core), mp: 4 (over z).
Axes of the slice: x: 2, y: 2, z: 4, core: 2. Of those that a mesh axis runs over, the one named last changes fastest.
Arguments:
- patches: bfloat16 [1024, 12800], P(('group', 'mp'), 'dp'), may hold values from -6 to 6
- norm_gain: float32 [12800], P('dp'), may hold values from 0.25 to 1.75
- norm_bias: float32 [12800], P('dp'), may hold values from -3 to 3
- proj_in: bfloat16 [12800, 4096], P('dp', ('group', 'mp')), may hold values from -0.0546875 to 0.0546875
- proj_in_bias: float32 [4096], P(('group', 'mp')), may hold values from -3 to 3
- proj_out: bfloat16 [4096, 4096], P(('group', 'mp'), 'dp'), may hold values from -0.09375 to 0.09375
- proj_out_bias: float32 [4096], P('dp'), may hold values from -3 to 3
- text_rows: bfloat16 [1024, 4096], P(('group', 'mp'), 'dp'), may hold values from -6 to 6
- out_grads: bfloat16 [1024, 4096], P(('group', 'mp'), 'dp'), may hold values from -6 to 6
- gate_weight: bfloat16 [4096, 14336], P('dp', 'mp'), may hold values from -0.09375 to 0.09375
- up_weight: bfloat16 [4096, 14336], P('dp', 'mp'), may hold values from -0.09375 to 0.09375
- down_weight: bfloat16 [14336, 4096], P('mp', 'dp'), may hold values from -0.046875 to 0.046875
- image_counts: int32 [16], replicated, may hold values from 16 to 64, as said below
- image_sequence: int32 [16], replicated, may hold values from 0 to 7, as said below
- image_offsets: int32 [16], replicated, may hold values from 0 to 112, as said below
Outputs:
- projected: bfloat16 [1024, 4096], P(('group', 'mp'), 'dp')
- sequence_grads: bfloat16 [1024, 4096], P(('group', 'mp'), 'dp')
- row_grads: bfloat16 [1024, 4096], P(('group', 'mp'), 'dp')
Inputs may be any that keep to these rules, and one draw needn't show every extreme that they name: `image_counts`: image rows lie end to end from row 0 in image order; rows after the last image belong to no image. `image_sequence`: every sequence holds exactly two images. `image_offsets`: the two images of a sequence do not intersect and lie within its 128 rows.
All inputs are finite; a program needn't handle non-finite values.
Results may differ from a plain program's by a relative error of at most 0.0075.
Values may be sent and summed in bfloat16 or wider, within the bound.
A program may use at most 192 MiB of HBM per device.

v0:
```python
import jax
import jax.numpy as jnp
from jax import lax
from jax.sharding import PartitionSpec as P

FEAT = 12800
TOK_DEV = 128


def seq_sources(counts, sequence, offsets, length, first, count):
    starts = jnp.cumsum(counts) - counts
    rows = first + jnp.arange(count, dtype=jnp.int32)
    seq = rows // length
    pos = rows % length
    hit = (
        (sequence[None, :] == seq[:, None])
        & (offsets[None, :] <= pos[:, None])
        & (pos[:, None] < (offsets + counts)[None, :])
    )
    source = jnp.sum(jnp.where(hit, starts[None, :] + pos[:, None] - offsets[None, :], 0), axis=1)
    return (source, jnp.any(hit, axis=1))


def image_targets(counts, sequence, offsets, length, first, count):
    starts = jnp.cumsum(counts) - counts
    rows = first + jnp.arange(count, dtype=jnp.int32)
    hit = (starts[None, :] <= rows[:, None]) & (rows[:, None] < (starts + counts)[None, :])
    target = jnp.sum(
        jnp.where(
            hit, sequence[None, :] * length + offsets[None, :] + rows[:, None] - starts[None, :], 0
        ),
        axis=1,
    )
    return (target, jnp.any(hit, axis=1))


def unit_grads(gate, up, hidden_grad):
    sig = jax.nn.sigmoid(gate)
    gate_grad = (hidden_grad * up * sig * (1.0 + gate * (1.0 - sig))).astype(jnp.bfloat16)
    up_grad = (hidden_grad * gate * sig).astype(jnp.bfloat16)
    return (gate_grad, up_grad)


def local(
    patches,
    norm_gain,
    norm_bias,
    proj_in,
    proj_in_bias,
    proj_out,
    proj_out_bias,
    text_rows,
    out_grads,
    gate_weight,
    up_weight,
    down_weight,
    image_counts,
    image_sequence,
    image_offsets,
):
    local_rows = patches.shape[0]
    values = patches.astype(jnp.float32)
    mean = lax.psum(jnp.sum(values, axis=1), "dp") / FEAT
    centred = values - mean[:, None]
    spread = lax.psum(jnp.sum(centred * centred, axis=1), "dp") / FEAT
    normed = (centred * lax.rsqrt(spread + 1e-05)[:, None] * norm_gain + norm_bias).astype(
        jnp.bfloat16
    )
    normed_all = lax.all_gather(normed, ("group", "mp"), axis=0, tiled=True)
    block = normed_all
    first = lax.psum_scatter(
        jnp.dot(block, proj_in, preferred_element_type=jnp.float32),
        "dp",
        scatter_dimension=0,
        tiled=True,
    )
    activated = jax.nn.gelu(first + proj_in_bias, approximate=False).astype(jnp.bfloat16)
    activated_all = lax.all_gather(activated, "dp", axis=0, tiled=True)
    block = activated_all
    summed = lax.psum(jnp.dot(block, proj_out, preferred_element_type=jnp.float32), ("group", "mp"))
    projected_all = (summed + proj_out_bias).astype(jnp.bfloat16)
    projected = lax.dynamic_slice_in_dim(
        projected_all, lax.axis_index(("group", "mp")) * local_rows, local_rows, 0
    )
    seq_text, seq_cotangent = (
        lax.all_gather(text_rows, "mp", axis=0, tiled=True),
        lax.all_gather(out_grads, "mp", axis=0, tiled=True),
    )
    group_rows = seq_text.shape[0]
    first_row = lax.axis_index("group") * group_rows
    source, covered = seq_sources(
        image_counts, image_sequence, image_offsets, TOK_DEV, first_row, group_rows
    )
    inputs = jnp.where(covered[:, None], jnp.take(projected_all, source, axis=0), seq_text)
    weights_both = jnp.concatenate([gate_weight, up_weight], axis=1)
    width = gate_weight.shape[1]
    both = jnp.dot(inputs, weights_both, preferred_element_type=jnp.float32)
    back = lax.dot_general(
        seq_cotangent, down_weight, (((1,), (1,)), ((), ())), preferred_element_type=jnp.float32
    )
    terms = lax.psum_scatter(
        jnp.concatenate([both, back], axis=1), "dp", scatter_dimension=0, tiled=True
    )
    gate_grad, up_grad = unit_grads(
        terms[:, :width], terms[:, width : 2 * width], terms[:, 2 * width :]
    )
    gate_all, up_all = (
        lax.all_gather(gate_grad, "dp", axis=0, tiled=True),
        lax.all_gather(up_grad, "dp", axis=0, tiled=True),
    )
    grads_all = jnp.concatenate([gate_all, up_all], axis=1)
    block = grads_all
    sequence_grads = lax.psum_scatter(
        lax.dot_general(
            block, weights_both, (((1,), (1,)), ((), ())), preferred_element_type=jnp.float32
        ),
        "mp",
        scatter_dimension=0,
        tiled=True,
    ).astype(jnp.bfloat16)
    returned = lax.all_gather(sequence_grads, ("group", "mp"), axis=0, tiled=True)
    target, valid = image_targets(
        image_counts,
        image_sequence,
        image_offsets,
        TOK_DEV,
        lax.axis_index(("group", "mp")) * local_rows,
        local_rows,
    )
    row_grads = jnp.where(
        valid[:, None], jnp.take(returned, target, axis=0), jnp.zeros((), jnp.bfloat16)
    )
    return (projected, sequence_grads, row_grads)


def solution(mesh):
    return jax.shard_map(
        local,
        mesh=mesh,
        in_specs=(
            P(("group", "mp"), "dp"),
            P("dp"),
            P("dp"),
            P("dp", ("group", "mp")),
            P(("group", "mp")),
            P(("group", "mp"), "dp"),
            P("dp"),
            P(("group", "mp"), "dp"),
            P(("group", "mp"), "dp"),
            P("dp", "mp"),
            P("dp", "mp"),
            P("mp", "dp"),
            P(),
            P(),
            P(),
        ),
        out_specs=(P(("group", "mp"), "dp"), P(("group", "mp"), "dp"), P(("group", "mp"), "dp")),
        check_vma=False,
    )
```

profile of v0, /device:TPU:0, one launch (start us, length us, event | category | flops | bytes accessed | tf_op | source)
XLA Modules:
  0.0 712.7 jit_solution(15998598072339114645)
XLA Ops:
  8.1 1.5 convert_reduce_fusion
  9.6 2.6 psum.21
  12.2 1.5 fusion.9
  13.7 2.5 psum.22
  16.2 2.5 fusion.12
  18.7 0.0 reduce-scatter.4.cloned.1.call-start
  18.7 159.7 %all-gather.7.cloned.1.call-done = bf16[1024,6400]{1,0:T(8,128)(2,1)} async-done(((bf16[64,6400]{1,0:T(8,128)(2,1)}), bf16[1024,6400]{1,0:T(8,128)(2,1)}) %all-gather.7.cloned.1.call-update) | async-done | bytes 13107216 | tf_op jit(solution)/shard_map/all_gather | solution.py:69
  178.4 7.7 %fusion.35 = f32[1024,256]{1,0:T(8,128)} fusion(bf16[1024,6400]{1,0:T(8,128)(2,1)} %all-gather.7.cloned.1.call-done, bf16[6400,256]{1,0:T(8,128)(2,1)S(1)} %copy-done), kind=kOutput, calls=%fused_computation.80 | convolution fusion | flops 3355443200 | bytes 17432576 | tf_op jit(solution)/shard_map/dot_general | solution.py:72
  186.1 0.0 all-gather.11.cloned.1.call-start
  186.2 0.5 all-gather.11.cloned.1.call-update
  186.7 0.0 all-reduce.2.cloned.1.call-start
  186.8 6.3 reduce-scatter.4.cloned.1.call-done
  193.0 2.2 fusion.20
  195.2 2.2 all_gather.22
  197.4 5.7 fusion.36
  203.2 0.0 all-gather.9.cloned.1.call-start
  203.2 0.5 all-gather.9.cloned.1.call-update
  203.7 0.2 reduce-scatter.6.cloned.1.call-start
  204.0 13.4 %constant_dynamic-update-slice_fusion.1 = bf16[2048,7168]{1,0:T(8,128)(2,1)} fusion(bf16[2048,3584]{1,0:T(8,128)(2,1)} %param.24), kind=kLoop, calls=%fused_computation.57 | loop fusion | bytes 29360128
  217.4 0.1 copy.20
  217.5 0.1 reduce
  217.7 0.1 fusion.34
  217.8 0.1 select_reduce_fusion
  217.9 13.2 %constant_dynamic-update-slice_fusion = bf16[2048,7168]{1,0:T(8,128)(2,1)} fusion(bf16[2048,7168]{1,0:T(8,128)(2,1)} %constant_dynamic-update-slice_fusion.1, bf16[2048,3584]{1,0:T(8,128)(2,1)} %param.25), kind=kLoop, calls=%fused_computation.56 | loop fusion | bytes 29360128 | tf_op jit(solution)/shard_map/concatenate | solution.py:95
  231.1 11.7 %fusion.37 = f32[256,3584]{1,0:T(8,128)} fusion(bf16[256,2048]{1,0:T(8,128)(2,1)} %all-gather.11.cloned.1.call-done, bf16[3584,2048]{1,0:T(8,128)(2,1)} %param.26), kind=kOutput, calls=%fused_computation.82 | convolution fusion | flops 3758096384 | bytes 19398656 | tf_op jit(solution)/shard_map/dot_general | solution.py:98
  242.7 236.0 %all-reduce.2.cloned.1.call-done = f32[1024,2048]{1,0:T(8,128)} async-done(((f32[1024,2048]{1,0:T(8,128)}), f32[1024,2048]{1,0:T(8,128)}) %all-reduce.2.cloned.1.call-update) | async-done | bytes 8388624 | tf_op jit(solution)/shard_map/psum | solution.py:80
  478.8 6.5 add_convert_fusion
  485.2 5.1 gather_fusion
  490.4 15.6 %fusion.13 = f32[256,7168]{1,0:T(8,128)} fusion(bf16[2048,7168]{1,0:T(8,128)(2,1)} %constant_dynamic-update-slice_fusion, bf16[256,2048]{1,0:T(8,128)(2,1)} %all-gather.9.cloned.1.call-done, bf16[256,2048]{1,0:T(8,128)(2,1)S(1)} %gather_fusion, pred[256]{0:T(512)(128)(4,1)S(1)} %compare_and_fusion.3, pred[256]{0:T(512)(128)(4,1)S(1)} %fusion.34), kind=kOutput, calls=%fused_computation.22 | convolution fusion | flops 7517241344 | bytes 38797824 | tf_op jit(solution)/shard_map/dot_general | solution.py:97
  505.9 9.2 %pad_maximum_fusion = f32[256,10752]{1,0:T(8,128)} fusion(f32[256,3584]{1,0:T(8,128)} %fusion.37, f32[256,7168]{1,0:T(8,128)} %fusion.13), kind=kLoop, calls=%fused_computation.2 | loop fusion | flops 2752512 | bytes 22020096 | tf_op jit(solution)/shard_map/concatenate | solution.py:102
  515.1 0.3 all-gather.15.cloned.1.call-start
  515.4 18.5 %reduce-scatter.6.cloned.1.call-done = f32[128,10752]{1,0:T(8,128)} async-done(((f32[256,10752]{1,0:T(8,128)}), f32[128,10752]{1,0:T(8,128)}) %reduce-scatter.6.cloned.1.call-update) | async-done | bytes 5505040 | tf_op jit(solution)/shard_map/reduce_scatter | solution.py:101
  533.8 4.8 fusion.8
  538.7 0.0 all-gather.13.cloned.1.call-start
  538.7 0.5 all-gather.13.cloned.1.call-update
  539.2 0.0 reduce-scatter.8.cloned.1.call-start
  539.3 11.0 %all-gather.15.cloned.1.call-done = bf16[256,3584]{1,0:T(8,128)(2,1)} async-done(((bf16[128,3584]{1,0:T(8,128)(2,1)}), bf16[256,3584]{1,0:T(8,128)(2,1)}) %all-gather.15.cloned.1.call-update) | async-done | bytes 1835024 | tf_op jit(solution)/shard_map/all_gather | solution.py:109
  550.2 12.9 %all-gather.13.cloned.1.call-done = bf16[256,3584]{1,0:T(8,128)(2,1)} async-done(((bf16[128,3584]{1,0:T(8,128)(2,1)}), bf16[256,3584]{1,0:T(8,128)(2,1)}) %all-gather.13.cloned.1.call-update) | async-done | bytes 1835024 | tf_op jit(solution)/shard_map/all_gather | solution.py:108
  563.1 15.6 %fusion = f32[256,2048]{1,0:T(8,128)} fusion(bf16[2048,7168]{1,0:T(8,128)(2,1)} %constant_dynamic-update-slice_fusion, bf16[256,3584]{1,0:T(8,128)(2,1)} %all-gather.15.cloned.1.call-done, bf16[256,3584]{1,0:T(8,128)(2,1)} %all-gather.13.cloned.1.call-done), kind=kOutput, calls=%fused_computation.4 | convolution fusion | flops 7523532800 | bytes 35127296 | tf_op jit(solution)/shard_map/dot_general | solution.py:114
  578.8 0.0 all-gather.17.cloned.1.call-start
  578.8 44.7 %reduce-scatter.8.cloned.1.call-done = f32[64,2048]{1,0:T(8,128)} async-done(((f32[256,2048]{1,0:T(8,128)}), f32[64,2048]{1,0:T(8,128)}) %reduce-scatter.8.cloned.1.call-update) | async-done | bytes 524304 | tf_op jit(solution)/shard_map/reduce_scatter | solution.py:113
  623.5 1.8 convert_element_type.27
  625.3 0.1 select_reduce_fusion.1
  625.4 0.1 fusion.29
  625.5 1.7 constant_dynamic-slice_fusion
  627.2 73.4 %all-gather.17.cloned.1.call-done = bf16[1024,2048]{1,0:T(8,128)(2,1)} async-done(((bf16[64,2048]{1,0:T(8,128)(2,1)}), bf16[1024,2048]{1,0:T(8,128)(2,1)}) %all-gather.17.cloned.1.call-update) | async-done | bytes 4194320 | tf_op jit(solution)/shard_map/all_gather | solution.py:121
  700.6 3.7 gather_fusion.1
  704.3 0.8 select_select_fusion
  (36 shorter events, 0.3 us)
Async XLA Ops:
  8.0 170.4 %copy-start = (bf16[6400,256]{1,0:T(8,128)(2,1)S(1)}, bf16[6400,256]{1,0:T(8,128)(2,1)}, u32[]{:S(2)}) copy-start(bf16[6400,256]{1,0:T(8,128)(2,1)} %param.18) | copy-start | bytes 9830404
  8.0 170.4 %all-gather.7.cloned.1.call-start = ((), (), s32[]{:S(2)}) async-start(), calls=%async_computation.3 | async-start | bytes 13926400 | tf_op jit(solution)/shard_map/all_gather | solution.py:69
  18.7 174.4 %copy-start.6 = (f32[256]{0:T(256)S(1)}, f32[256]{0:T(256)}, u32[]{:S(2)}) copy-start(f32[256]{0:T(256)} %param.19) | copy-start | bytes 3076
  18.7 174.3 %reduce-scatter.4.cloned.1.call-start = ((), (), s32[]{:S(2)}) async-start(), calls=%async_computation.4 | async-start | bytes 1572864 | tf_op jit(solution)/shard_map/reduce_scatter | solution.py:71
  186.1 45.0 %all-gather.11.cloned.1.call-start = ((), (), s32[]{:S(2)}) async-start(), calls=%async_computation.7 | async-start | bytes 1310720 | tf_op jit(solution)/shard_map/all_gather | solution.py:87
  186.7 292.1 %all-reduce.2.cloned.1.call-start = ((), (), s32[]{:S(2)}) async-start(), calls=%async_computation.5 | async-start | bytes 16777216 | tf_op jit(solution)/shard_map/psum | solution.py:80
  203.2 287.2 %all-gather.9.cloned.1.call-start = ((), (), s32[]{:S(2)}) async-start(), calls=%async_computation.6 | async-start | bytes 1310720 | tf_op jit(solution)/shard_map/all_gather | solution.py:86
  203.7 330.1 %reduce-scatter.6.cloned.1.call-start = ((), (), s32[]{:S(2)}) async-start(), calls=%async_computation.8 | async-start | bytes 16515072 | tf_op jit(solution)/shard_map/reduce_scatter | solution.py:101
  204.0 13.4 %copy-start.5 = (s32[16]{0:T(128)S(1)}, s32[16]{0:T(128)}, u32[]{:S(2)}) copy-start(s32[16]{0:T(128)} %param.27) | copy-start | bytes 196
  204.0 13.6 %copy-start.3 = (s32[16]{0:T(128)S(1)}, s32[16]{0:T(128)}, u32[]{:S(2)}) copy-start(s32[16]{0:T(128)} %param.29) | copy-start | bytes 196
  204.0 13.6 %copy-start.4 = (s32[16]{0:T(128)S(1)}, s32[16]{0:T(128)}, u32[]{:S(2)}) copy-start(s32[16]{0:T(128)} %param.28) | copy-start | bytes 196
  231.1 247.7 %copy-start.2 = (f32[2048]{0:T(1024)S(1)}, f32[2048]{0:T(1024)}, u32[]{:S(2)}) copy-start(f32[2048]{0:T(1024)} %param.21) | copy-start | bytes 24580
  515.1 35.1 %all-gather.15.cloned.1.call-start = ((), (), s32[]{:S(2)}) async-start(), calls=%async_computation.10 | async-start | bytes 2752512 | tf_op jit(solution)/shard_map/all_gather | solution.py:109
  538.7 24.5 %all-gather.13.cloned.1.call-start = ((), (), s32[]{:S(2)}) async-start(), calls=%async_computation.9 | async-start | bytes 2752512 | tf_op jit(solution)/shard_map/all_gather | solution.py:108
  539.2 84.3 %reduce-scatter.8.cloned.1.call-start = ((), (), s32[]{:S(2)}) async-start(), calls=%async_computation.11 | async-start | bytes 2621440 | tf_op jit(solution)/shard_map/reduce_scatter | solution.py:113
  563.1 142.0 %copy-start.1 = (bf16[6400,256]{1,0:T(8,128)(2,1)S(1)}, bf16[6400,256]{1,0:T(8,128)(2,1)}, u32[]{:S(2)}) copy-start(bf16[6400,256]{1,0:T(8,128)(2,1)} %param.18) | copy-start | bytes 9830404
  578.8 121.8 %all-gather.17.cloned.1.call-start = ((), (), s32[]{:S(2)}) async-start(), calls=%async_computation.12 | async-start | bytes 4456448 | tf_op jit(solution)/shard_map/all_gather | solution.py:121
Sparse Core Ops, SparseCore 0:
  18.8 159.5 all-gather.6
  186.2 6.7 reduce-scatter.3
  203.3 275.4 all-reduce.1
  515.2 18.5 reduce-scatter.5
  538.8 11.4 all-gather.14
  551.7 11.3 all-gather.12
  625.4 75.1 all-gather.16
Sparse Core Ops, SparseCore 1:
  188.2 34.4 all-gather.10
  224.2 55.4 all-gather.8
  578.8 44.6 reduce-scatter.7
where the time goes:
time: 713 us
  waiting for transfers between devices  564 us (79%)
  matrix products  56.3 us (8%)
  local copies, waits for them, and re-layouts  37.2 us (5%)
  other arithmetic  31.3 us (4%)
  between operations  15.9 us (2%)
  blocking collectives  7.25 us (1%)
    psum x1, waiting for transfers between devices, local(): lax.psum(jnp.dot(block, proj_out, preferred_element_type=jnp.float32), ('...  236 us
    all_gather x1, waiting for transfers between devices, local(): normed_all = lax.all_gather(normed, ('group', 'mp'), axis=0, tiled=True)  160 us
    all_gather x1, waiting for transfers between devices, local(): lax.all_gather(sequence_grads, ('group', 'mp'), axis=0, tiled=True)  73.4 us
    reduce_scatter x1, waiting for transfers between devices, local(): lax.psum_scatter(lax.dot_general(block, weights_both, (((1,), (1,)), ((),...  44.7 us
    reduce_scatter x1, waiting for transfers between devices, local(): lax.psum_scatter(jnp.concatenate([both, back], axis=1), 'dp', scatter_dim...  18.5 us
    dot_general x1, matrix products, local(): lax.dot_general(block, weights_both, (((1,), (1,)), ((), ())), preferred_...  15.6 us
    dot_general x1, matrix products, local(): both = jnp.dot(inputs, weights_both, preferred_element_type=jnp.float32)  15.6 us
  transfers between devices with their start and end apart: 10, of which 8 were waited for; matrix products, arithmetic and copies ran while one was open for 8% of the time, Pallas kernels for 0%

commit v1 on v0

v1 whole, which is shorter than its diff:
```python
import functools

import jax
import jax.numpy as jnp
from jax import lax
from jax.sharding import PartitionSpec as P

TOK_DEV = 128


def seq_sources(counts, sequence, offsets, length, first, count):
    starts = jnp.cumsum(counts) - counts
    rows = first + jnp.arange(count, dtype=jnp.int32)
    seq = rows // length
    pos = rows % length
    hit = (
        (sequence[None, :] == seq[:, None])
        & (offsets[None, :] <= pos[:, None])
        & (pos[:, None] < (offsets + counts)[None, :])
    )
    source = jnp.sum(jnp.where(hit, starts[None, :] + pos[:, None] - offsets[None, :], 0), axis=1)
    return (source, jnp.any(hit, axis=1))


def image_targets(counts, sequence, offsets, length, first, count):
    starts = jnp.cumsum(counts) - counts
    rows = first + jnp.arange(count, dtype=jnp.int32)
    hit = (starts[None, :] <= rows[:, None]) & (rows[:, None] < (starts + counts)[None, :])
    target = jnp.sum(
        jnp.where(
            hit, sequence[None, :] * length + offsets[None, :] + rows[:, None] - starts[None, :], 0
        ),
        axis=1,
    )
    return (target, jnp.any(hit, axis=1))


def unit_grads(gate, up, hidden_grad):
    sig = jax.nn.sigmoid(gate)
    gate_grad = (hidden_grad * up * sig * (1.0 + gate * (1.0 - sig))).astype(jnp.bfloat16)
    up_grad = (hidden_grad * gate * sig).astype(jnp.bfloat16)
    return (gate_grad, up_grad)


def swap_dp(value):
    return lax.ppermute(value, "dp", [(0, 1), (1, 0)])


def half_rows(value, part):
    rows = value.shape[0] // 2
    return lax.dynamic_slice_in_dim(value, part * rows, rows, 0)


def local(
    sizes,
    patches,
    norm_gain,
    norm_bias,
    proj_in,
    proj_in_bias,
    proj_out,
    proj_out_bias,
    text_rows,
    out_grads,
    gate_weight,
    up_weight,
    down_weight,
    image_counts,
    image_sequence,
    image_offsets,
):
    groups, dps, mps = sizes
    devices = groups * mps
    local_rows, local_cols = text_rows.shape
    total = local_rows * devices
    group_rows = local_rows * mps
    group, dp, mp = (lax.axis_index(a) for a in ("group", "dp", "mp"))
    bf16, f32 = jnp.bfloat16, jnp.float32
    rank = ("mp", "group")

    block = local_cols // devices
    out_cols = lax.all_to_all(proj_out, rank, 1, 0, tiled=True)
    out_cols = lax.all_gather(out_cols, "dp", axis=1, tiled=True)
    out_bias = lax.dynamic_slice_in_dim(proj_out_bias, (mp * groups + group) * block, block, 0)
    out_bias = lax.all_gather(out_bias, "dp", axis=0, tiled=True)

    seq_text, seq_cotangent = (
        lax.all_gather(text_rows, "mp", axis=0, tiled=True),
        lax.all_gather(out_grads, "mp", axis=0, tiled=True),
    )

    values = patches.astype(f32)
    mean = lax.psum(jnp.sum(values, axis=1), "dp") / (patches.shape[1] * dps)
    centred = values - mean[:, None]
    spread = lax.psum(jnp.sum(centred * centred, axis=1), "dp") / (patches.shape[1] * dps)
    normed = (centred * lax.rsqrt(spread + 1e-05)[:, None] * norm_gain + norm_bias).astype(bf16)
    normed_all = lax.all_gather(normed, ("group", "mp"), axis=0, tiled=True)

    def matmul(a, b):
        return jnp.dot(a, b, preferred_element_type=f32)

    def matmul_t(a, b):
        return lax.dot_general(a, b, (((1,), (1,)), ((), ())), preferred_element_type=f32)

    def summed_share(value, op):
        if dps == 2:
            arriving = swap_dp(op(half_rows(value, 1 - dp)))
            return op(half_rows(value, dp)) + arriving
        return lax.psum_scatter(op(value), "dp", scatter_dimension=0, tiled=True)

    hidden_grad = summed_share(seq_cotangent, lambda rows: matmul_t(rows, down_weight))

    first = summed_share(normed_all, lambda rows: matmul(rows, proj_in))
    activated = jax.nn.gelu(first + proj_in_bias, approximate=False).astype(bf16)
    activated_all = lax.all_gather(activated, rank, axis=1, tiled=True)
    columns = (matmul(activated_all, out_cols) + out_bias).astype(bf16)
    columns = lax.all_to_all(columns, "dp", 1, 0, tiled=True)

    source, covered = seq_sources(
        image_counts, image_sequence, image_offsets, TOK_DEV, 0, total
    )
    placed = jnp.take(columns, source, axis=0)
    placed = lax.all_to_all(placed, "group", 0, 1, tiled=True)
    placed = lax.all_gather(placed, "mp", axis=1, tiled=True)
    covered = lax.dynamic_slice_in_dim(covered, group * group_rows, group_rows, 0)
    inputs = jnp.where(covered[:, None], placed, seq_text)

    by_rank = columns.reshape(groups, mps, local_rows, -1).swapaxes(0, 1).reshape(total, -1)
    projected = lax.all_to_all(by_rank, rank, 0, 1, tiled=True)

    up = summed_share(inputs, lambda rows: matmul(rows, up_weight))
    gate = summed_share(inputs, lambda rows: matmul(rows, gate_weight))
    gate_grad, up_grad = unit_grads(gate, up, hidden_grad)

    def back(gate_rows, up_rows):
        return (matmul_t(gate_rows, gate_weight) + matmul_t(up_rows, up_weight)).astype(bf16)

    if dps == 2:
        gate_other, up_other = swap_dp(gate_grad), swap_dp(up_grad)
        mine = back(gate_grad, up_grad)
        other = back(gate_other, up_other)
        partial = jnp.where(
            dp == 0, jnp.concatenate([mine, other], 0), jnp.concatenate([other, mine], 0)
        )
    else:
        partial = back(
            lax.all_gather(gate_grad, "dp", axis=0, tiled=True),
            lax.all_gather(up_grad, "dp", axis=0, tiled=True),
        )
    share = local_cols // mps
    shares = lax.all_to_all(
        partial.reshape(group_rows, mps, share).swapaxes(0, 1), "mp", 0, 0, tiled=True
    )
    grads = jnp.sum(shares.astype(f32), axis=0).astype(bf16)

    grads_all = lax.all_gather(grads, "group", axis=0, tiled=True)
    target, valid = image_targets(
        image_counts,
        image_sequence,
        image_offsets,
        TOK_DEV,
        group * group_rows,
        group_rows,
    )
    rows = jnp.where(valid[:, None], jnp.take(grads_all, target, axis=0), jnp.zeros((), bf16))
    row_grads = lax.all_to_all(rows, "mp", 0, 1, tiled=True)
    sequence_grads = lax.all_to_all(grads, "mp", 0, 1, tiled=True)
    return (projected, sequence_grads, row_grads)


def solution(mesh):
    sizes = tuple(mesh.shape[a] for a in ("group", "dp", "mp"))
    return jax.shard_map(
        functools.partial(local, sizes),
        mesh=mesh,
        in_specs=(
            P(("group", "mp"), "dp"),
            P("dp"),
            P("dp"),
            P("dp", ("group", "mp")),
            P(("group", "mp")),
            P(("group", "mp"), "dp"),
            P("dp"),
            P(("group", "mp"), "dp"),
            P(("group", "mp"), "dp"),
            P("dp", "mp"),
            P("dp", "mp"),
            P("mp", "dp"),
            P(),
            P(),
            P(),
        ),
        out_specs=(P(("group", "mp"), "dp"), P(("group", "mp"), "dp"), P(("group", "mp"), "dp")),
        check_vma=False,
    )
```

time: 713 us -> 558 us (0.78)
  waiting for transfers between devices: 564 us -> 284 us
  blocking collectives: 7.25 us -> 102 us
  matrix products: 56.3 us -> 114 us
  other arithmetic: 31.3 us -> 10.2 us
  local copies, waits for them, and re-layouts: 37.2 us -> 17.3 us
  starting transfers between devices: 0.82 us -> 15 us
    psum x1 -> x0, waiting for transfers between devices: 236 us -> none  [local(): lax.psum(jnp.dot(block, proj_out, preferred_element_type=jnp.float32), ('...]
    all_to_all x0 -> x4, blocking collectives: none -> 94.9 us  [the longest x1 52.5 us: local(): out_cols = lax.all_to_all(proj_out, rank, 1, 0, tiled=True)]
    reduce_scatter x3 -> x0, waiting for transfers between devices: 69.4 us -> none  [the longest x1 44.7 us: local(): lax.psum_scatter(lax.dot_general(block, weights_both, (((1,), (1,)), ((),...]
    dot_general x5 -> x13, matrix products: 56.3 us -> 114 us  [the longest x6 64.8 us: matmul_t(): lax.dot_general(a, b, (((1,), (1,)), ((), ())), preferred_element_type=f32)]
    all_gather x1, waiting for transfers between devices: 160 us -> 122 us  [local(): normed_all = lax.all_gather(normed, ('group', 'mp'), axis=0, tiled=True)]
    all_gather x3 -> x4, waiting for transfers between devices: 97.2 us -> 121 us  [the longest x1 83.5 us: local(): activated_all = lax.all_gather(activated, rank, axis=1, tiled=True)]
    all_gather x1, waiting for transfers between devices: 0.01 us -> 18.6 us  [local(): lax.all_gather(out_grads, 'mp', axis=0, tiled=True)]
    convert_element_type x4 -> x0, other arithmetic: 15.2 us -> none  [the longest x1 6.47 us: local(): projected_all = (summed + proj_out_bias).astype(jnp.bfloat16)]
  transfers between devices with their start and end apart: 10 -> 16, of which waited for: 8 -> 9; matrix products, arithmetic and copies ran while one was open for 8% -> 19% of each run, Pallas kernels for 0% -> 0%
where the time goes in v1:
time: 558 us; the launch traced here: 557 us
  waiting for transfers between devices  284 us (51%)
  matrix products  114 us (20%)
  blocking collectives  102 us (18%)
  local copies, waits for them, and re-layouts  17.3 us (3%)
  starting transfers between devices  15 us (3%)
  between operations  14.4 us (3%)
  other arithmetic  10.2 us (2%)
    all_gather x1, waiting for transfers between devices, local(): normed_all = lax.all_gather(normed, ('group', 'mp'), axis=0, tiled=True)  122 us
    all_gather x1, waiting for transfers between devices, local(): activated_all = lax.all_gather(activated, rank, axis=1, tiled=True)  83.5 us
    dot_general x6, matrix products, matmul_t(): lax.dot_general(a, b, (((1,), (1,)), ((), ())), preferred_element_type=f32)  64.8 us
    all_to_all x1, blocking collectives, local(): out_cols = lax.all_to_all(proj_out, rank, 1, 0, tiled=True)  52.5 us
    dot_general x7, matrix products, matmul(): return jnp.dot(a, b, preferred_element_type=f32)  49.7 us
    all_gather x1, waiting for transfers between devices, local(): placed = lax.all_gather(placed, 'mp', axis=1, tiled=True)  29.4 us
    all_to_all x1, blocking collectives, local(): lax.all_to_all(partial.reshape(group_rows, mps, share).swapaxes(0, 1), 'm...  29 us
    all_gather x1, waiting for transfers between devices, local(): lax.all_gather(out_grads, 'mp', axis=0, tiled=True)  18.6 us
  transfers between devices with their start and end apart: 16, of which 9 were waited for; matrix products, arithmetic and copies ran while one was open for 19% of the time, Pallas kernels for 0%

profile of v1, /device:TPU:0, one launch (start us, length us, event | category | flops | bytes accessed | tf_op | source)
XLA Modules:
  0.0 557.1 jit_solution(2403520004139355009)
XLA Ops:
  7.2 1.5 convert_reduce_fusion
  8.7 2.6 psum.14
  11.3 1.5 fusion.12
  12.9 2.5 psum.15
  15.3 2.4 fusion.15
  17.8 2.3 copy.58
  20.1 52.5 %all_to_all.113 = bf16[256,16,128]{0,2,1:T(8,128)(2,1)} all-to-all(bf16[256,16,128]{0,2,1:T(8,128)(2,1)} %bitcast.73), channel_id=1, replica_groups=mesh['group'=4,'dp'=2,'mp'=4] {'mp','group'}, dimensions={1} | all-to-all | bytes 2097152 | tf_op jit(solution)/shard_map/all_to_all | solution.py:82
  72.6 2.3 copy.59
  75.0 121.5 %all-gather.9.cloned.1.call-done = bf16[1024,6400]{1,0:T(8,128)(2,1)} async-done(((bf16[64,6400]{1,0:T(8,128)(2,1)}), bf16[1024,6400]{1,0:T(8,128)(2,1)}) %all-gather.9.cloned.1.call-update) | async-done | bytes 13107216 | tf_op jit(solution)/shard_map/all_gather | solution.py:97
  196.5 5.5 fusion
  202.0 2.2 collective-permute-done
  204.3 6.8 %fusion.26 = bf16[512,256]{1,0:T(8,128)(2,1)} fusion(f32[512,256]{1,0:T(8,128)} %collective-permute-done, bf16[6400,256]{1,0:T(8,128)(2,1)S(1)} %copy-done, bf16[1024,6400]{1,0:T(8,128)(2,1)} %all-gather.9.cloned.1.call-done, s32[]{:T(128)S(6)} %select_n.115, f32[256]{0:T(256)S(1)} %copy-done.7), kind=kOutput, calls=%fused_computation.37 | convolution fusion | flops 1686503424 | bytes 10617860 | tf_op jit(solution)/shard_map/dot_general | solution.py:100
  211.7 0.8 dynamic-slice_bitcast_fusion
  212.5 1.8 all-gather
  214.7 83.5 %all-gather.11.cloned.1.call-done = bf16[512,4096]{1,0:T(8,128)(2,1)} async-done(((bf16[512,256]{1,0:T(8,128)(2,1)}), bf16[512,4096]{1,0:T(8,128)(2,1)}) %all-gather.11.cloned.1.call-update) | async-done | bytes 4194320 | tf_op jit(solution)/shard_map/all_gather | solution.py:115
  298.2 4.2 fusion.22
  302.6 3.9 all_to_all.114
  306.5 3.2 gather_fusion
  309.9 9.5 %all_to_all.115 = bf16[4,256,128]{2,1,0:T(8,128)(2,1)S(1)} all-to-all(bf16[4,256,128]{2,1,0:T(8,128)(2,1)S(1)} %broadcast_select_fusion.1), channel_id=1, replica_groups=mesh['group'=4,'dp'=2,'mp'=4] {'group'}, dimensions={0} | all-to-all | bytes 524288 | tf_op jit(solution)/shard_map/all_to_all | solution.py:123
  319.4 0.7 copy_bitcast_fusion.2
  321.2 4.6 all-gather.19.cloned.1.call-done
  325.8 29.4 %all-gather.17.cloned.1.call-done = bf16[256,2048]{1,0:T(8,128)(2,1)} async-done(((bf16[256,512]{1,0:T(8,128)(2,1)}), bf16[256,2048]{1,0:T(8,128)(2,1)}) %all-gather.17.cloned.1.call-update) | async-done | bytes 1048592 | tf_op jit(solution)/shard_map/all_gather | solution.py:124
  355.3 1.7 broadcast_select_fusion
  357.0 8.5 %fusion.39 = f32[128,3584]{1,0:T(8,128)} fusion(bf16[2048,3584]{1,0:T(8,128)(2,1)} %param.24, bf16[256,2048]{1,0:T(8,128)(2,1)S(1)} %broadcast_select_fusion, s32[]{:T(128)S(6)} %select_n.120), kind=kOutput, calls=%fused_computation.58 | convolution fusion | flops 1879048192 | bytes 17039364 | tf_op jit(solution)/shard_map/dot_general | solution.py:100
  365.5 18.6 %all-gather.15.cloned.1.call-done = bf16[256,2048]{1,0:T(8,128)(2,1)} async-done(((bf16[64,2048]{1,0:T(8,128)(2,1)}), bf16[256,2048]{1,0:T(8,128)(2,1)}) %all-gather.15.cloned.1.call-update) | async-done | bytes 1048592 | tf_op jit(solution)/shard_map/all_gather | solution.py:89
  384.2 11.5 %fusion.27 = f32[128,3584]{1,0:T(8,128)} fusion(bf16[3584,2048]{1,0:T(8,128)(2,1)} %param.26, bf16[256,2048]{1,0:T(8,128)(2,1)} %all-gather.15.cloned.1.call-done, s32[]{:T(128)S(6)} %select_n.120), kind=kOutput, calls=%fused_computation.40 | convolution fusion | flops 1879048192 | bytes 17039364 | tf_op jit(solution)/shard_map/dot_general | solution.py:103
  395.7 7.2 %fusion.41 = f32[128,3584]{1,0:T(8,128)S(1)} fusion(bf16[2048,3584]{1,0:T(8,128)(2,1)} %param.25, bf16[256,2048]{1,0:T(8,128)(2,1)S(1)} %broadcast_select_fusion, s32[]{:T(128)S(6)} %select_n.120), kind=kOutput, calls=%fused_computation.60 | convolution fusion | flops 1879048192 | bytes 17039364 | tf_op jit(solution)/shard_map/dot_general | solution.py:100
  403.5 8.5 %convolution_add_fusion = f32[128,3584]{1,0:T(8,128)} fusion(f32[128,3584]{1,0:T(8,128)S(1)} %collective-permute-done.3, bf16[2048,3584]{1,0:T(8,128)(2,1)} %param.24, bf16[256,2048]{1,0:T(8,128)(2,1)S(1)} %broadcast_select_fusion, s32[]{:T(128)S(6)} %select_n.119), kind=kOutput, calls=%fused_computation.6 | convolution fusion | flops 1879506944 | bytes 18874372 | tf_op jit(solution)/shard_map/dot_general | solution.py:100
  412.1 13.3 %multiply_convert_fusion = (bf16[128,3584]{1,0:T(8,128)(2,1)}, f32[128,3584]{1,0:T(8,128)}) fusion(f32[128,3584]{1,0:T(8,128)} %convolution_add_fusion, f32[128,3584]{1,0:T(8,128)} %collective-permute-done.1, bf16[3584,2048]{1,0:T(8,128)(2,1)} %param.26, bf16[256,2048]{1,0:T(8,128)(2,1)} %all-gather.15.cloned.1.call-done, s32[]{:T(128)S(6)} %select_n.119), kind=kOutput, calls=%fused_computation.21 | convolution fusion | flops 1882259456 | bytes 21626884 | tf_op jit(solution)/shard_map/dot_general | solution.py:103
  425.4 8.9 %fusion.7 = bf16[128,3584]{1,0:T(8,128)(2,1)S(1)} fusion(f32[128,3584]{1,0:T(8,128)} %get-tuple-element.7, f32[128,3584]{1,0:T(8,128)} %collective-permute-done.2, bf16[2048,3584]{1,0:T(8,128)(2,1)} %param.25, f32[128,3584]{1,0:T(8,128)S(1)} %copy-done.2, bf16[256,2048]{1,0:T(8,128)(2,1)S(1)} %broadcast_select_fusion, s32[]{:T(128)S(6)} %select_n.119), kind=kOutput, calls=%fused_computation.12 | convolution fusion | flops 1884094464 | bytes 21626884 | tf_op jit(solution)/shard_map/dot_general | solution.py:100
  434.3 10.0 %fusion.62 = f32[128,2048]{1,0:T(8,128)S(1)} fusion(bf16[128,3584]{1,0:T(8,128)(2,1)S(1)} %fusion.7, bf16[2048,3584]{1,0:T(8,128)(2,1)} %param.24), kind=kOutput, calls=%fused_computation.106 | convolution fusion | flops 1879048192 | bytes 16646144 | tf_op jit(solution)/shard_map/dot_general | solution.py:103
  444.8 9.9 %fusion.8 = bf16[128,2048]{1,0:T(8,128)(2,1)S(1)} fusion(f32[128,2048]{1,0:T(8,128)S(1)} %fusion.62, bf16[128,3584]{1,0:T(8,128)(2,1)S(1)} %copy-done.3, bf16[2048,3584]{1,0:T(8,128)(2,1)} %param.25), kind=kOutput, calls=%fused_computation.15 | convolution fusion | flops 1879572480 | bytes 17170432 | tf_op jit(solution)/shard_map/dot_general | solution.py:103
  454.8 9.9 %fusion.63 = f32[128,2048]{1,0:T(8,128)S(1)} fusion(bf16[128,3584]{1,0:T(8,128)(2,1)S(1)} %collective-permute-done.5, bf16[2048,3584]{1,0:T(8,128)(2,1)} %param.25), kind=kOutput, calls=%fused_computation.107 | convolution fusion | flops 1879048192 | bytes 16646144 | tf_op jit(solution)/shard_map/dot_general | solution.py:103
  464.8 10.2 %fusion.9 = bf16[128,2048]{1,0:T(8,128)(2,1)S(1)} fusion(f32[128,2048]{1,0:T(8,128)S(1)} %fusion.63, bf16[128,3584]{1,0:T(8,128)(2,1)S(1)} %collective-permute-done.4, bf16[2048,3584]{1,0:T(8,128)(2,1)} %param.24), kind=kOutput, calls=%fused_computation.16 | convolution fusion | flops 1879572480 | bytes 17170432 | tf_op jit(solution)/shard_map/dot_general | solution.py:103
  475.4 29.0 %all_to_all.116 = bf16[4,256,512]{2,1,0:T(8,128)(2,1)S(1)} all-to-all(bf16[4,256,512]{2,1,0:T(8,128)(2,1)S(1)} %fusion.23), channel_id=1, replica_groups=mesh['group'=4,'dp'=2,'mp'=4] {'mp'}, dimensions={0} | all-to-all | bytes 2097152 | tf_op jit(solution)/shard_map/all_to_all | solution.py:151
  504.4 0.9 reduce_sum.61
  505.3 0.7 copy.61
  506.1 4.7 all-to-all-start.2
  511.0 9.2 %all-to-all-done.2 = bf16[16,64,128]{2,1,0:T(8,128)(2,1)} async-done(((bf16[16,64,128]{2,1,0:T(8,128)(2,1)}), bf16[16,64,128]{2,1,0:T(8,128)(2,1)}, u32[]{:S(2)}, u32[]{:S(2)}) %all-to-all-start.2) | async-done | bytes 262176 | tf_op jit(solution)/shard_map/all_to_all | solution.py:129
  520.2 4.0 all-to-all-start.5
  524.4 8.1 %all-gather.21.cloned.1.call-done = bf16[1024,512]{1,0:T(8,128)(2,1)} async-done(((bf16[256,512]{1,0:T(8,128)(2,1)}), bf16[1024,512]{1,0:T(8,128)(2,1)}) %all-gather.21.cloned.1.call-update) | async-done | bytes 1048592 | tf_op jit(solution)/shard_map/all_gather | solution.py:156
  532.6 2.6 gather_fusion.1
  535.1 0.8 select_select_fusion
  536.0 4.6 all-to-all-start.6
  540.6 1.7 copy_bitcast_fusion.3
  542.3 1.7 copy.75
  543.9 5.6 all-to-all-done.6
  549.5 0.7 copy.76
  (70 shorter events, 4.7 us)
Async XLA Ops:
  7.2 189.3 %copy-start = (bf16[6400,256]{1,0:T(8,128)(2,1)S(1)}, bf16[6400,256]{1,0:T(8,128)(2,1)}, u32[]{:S(2)}) copy-start(bf16[6400,256]{1,0:T(8,128)(2,1)} %param.18) | copy-start | bytes 9830404
  7.2 189.3 %all-gather.9.cloned.1.call-start = ((), (), s32[]{:S(2)}) async-start(), calls=%async_computation.7 | async-start | bytes 13926400 | tf_op jit(solution)/shard_map/all_gather | solution.py:97
  17.8 196.9 %all-gather.13.cloned.1.call-start = ((), (), s32[]{:S(2)}) async-start(), calls=%async_computation.9 | async-start | bytes 3145728 | tf_op jit(solution)/shard_map/all_gather | solution.py:83
  74.9 223.3 %all-gather.11.cloned.1.call-start = ((), (), s32[]{:S(2)}) async-start(), calls=%async_computation.8 | async-start | bytes 4456448 | tf_op jit(solution)/shard_map/all_gather | solution.py:115
  75.0 129.3 %copy-start.7 = (f32[256]{0:T(256)S(1)}, f32[256]{0:T(256)}, u32[]{:S(2)}) copy-start(f32[256]{0:T(256)} %param.19) | copy-start | bytes 3076
  202.0 2.3 collective-permute-start
  202.0 12.2 %copy-start.6 = (s32[16]{0:T(128)S(1)}, s32[16]{0:T(128)}, u32[]{:S(2)}) copy-start(s32[16]{0:T(128)} %param.27) | copy-start | bytes 196
  202.0 12.5 %copy-start.4 = (s32[16]{0:T(128)S(1)}, s32[16]{0:T(128)}, u32[]{:S(2)}) copy-start(s32[16]{0:T(128)} %param.29) | copy-start | bytes 196
  202.0 12.5 %copy-start.5 = (s32[16]{0:T(128)S(1)}, s32[16]{0:T(128)}, u32[]{:S(2)}) copy-start(s32[16]{0:T(128)} %param.28) | copy-start | bytes 196
  211.1 114.7 %all-gather.19.cloned.1.call-start = ((), (), s32[]{:S(2)}) async-start(), calls=%async_computation.12 | async-start | bytes 1310720 | tf_op jit(solution)/shard_map/all_gather | solution.py:88
  211.7 143.6 %all-gather.17.cloned.1.call-start = ((), (), s32[]{:S(2)}) async-start(), calls=%async_computation.11 | async-start | bytes 1310720 | tf_op jit(solution)/shard_map/all_gather | solution.py:124
  320.2 64.0 %all-gather.15.cloned.1.call-start = ((), (), s32[]{:S(2)}) async-start(), calls=%async_computation.10 | async-start | bytes 1310720 | tf_op jit(solution)/shard_map/all_gather | solution.py:89
  320.8 211.8 %all-gather.21.cloned.1.call-start = ((), (), s32[]{:S(2)}) async-start(), calls=%async_computation.13 | async-start | bytes 1310720 | tf_op jit(solution)/shard_map/all_gather | solution.py:156
  365.5 38.0 %collective-permute-start.3 = (f32[128,3584]{1,0:T(8,128)}, f32[128,3584]{1,0:T(8,128)S(1)}, u32[]{:S(2)}, u32[]{:S(2)}) collective-permute-start(f32[128,3584]{1,0:T(8,128)} %fusion.39), channel_id=1, source_target_pairs={{0,4},{4,0},{1,5},{5,1},{2,6},{6,2},{3,7},{7,3},{8,12},{12,8},{9,1... | collective-permute-start | bytes 5505032 | tf_op jit(solution)/shard_map/ppermute | solution.py:46
  395.7 16.4 %collective-permute-start.1 = (f32[128,3584]{1,0:T(8,128)}, f32[128,3584]{1,0:T(8,128)}, u32[]{:S(2)}, u32[]{:S(2)}) collective-permute-start(f32[128,3584]{1,0:T(8,128)} %fusion.27), channel_id=1, source_target_pairs={{0,4},{4,0},{1,5},{5,1},{2,6},{6,2},{3,7},{7,3},{8,12},{12,8},{9,1... | collective-permute-start | bytes 5505032 | tf_op jit(solution)/shard_map/ppermute | solution.py:46
  403.0 22.4 %collective-permute-start.2 = (f32[128,3584]{1,0:T(8,128)S(1)}, f32[128,3584]{1,0:T(8,128)}, u32[]{:S(2)}, u32[]{:S(2)}) collective-permute-start(f32[128,3584]{1,0:T(8,128)S(1)} %fusion.41), channel_id=1, source_target_pairs={{0,4},{4,0},{1,5},{5,1},{2,6},{6,2},{3,7},{7,3},{8,12},{12,8},{9,1... | collective-permute-start | bytes 5505032 | tf_op jit(solution)/shard_map/ppermute | solution.py:46
  412.1 13.3 %copy-start.2 = (f32[128,3584]{1,0:T(8,128)S(1)}, f32[128,3584]{1,0:T(8,128)}, u32[]{:S(2)}) copy-start(f32[128,3584]{1,0:T(8,128)} %convolution_add_fusion) | copy-start | bytes 5505028
  434.3 10.1 %copy-start.3 = (bf16[128,3584]{1,0:T(8,128)(2,1)S(1)}, bf16[128,3584]{1,0:T(8,128)(2,1)}, u32[]{:S(2)}) copy-start(bf16[128,3584]{1,0:T(8,128)(2,1)} %get-tuple-element.6) | copy-start | bytes 2752516
  444.3 20.5 %collective-permute-start.4 = (bf16[128,3584]{1,0:T(8,128)(2,1)S(1)}, bf16[128,3584]{1,0:T(8,128)(2,1)S(1)}, u32[]{:S(2)}, u32[]{:S(2)}) collective-permute-start(bf16[128,3584]{1,0:T(8,128)(2,1)S(1)} %fusion.7), channel_id=1, source_target_pairs={{0,4},{4,0},{1,5},{5,1},{2,6},{6,2},{3,7},{7,3},{8,12},{12,8},{9,1... | collective-permute-start | bytes 2752520 | tf_op jit(solution)/shard_map/ppermute | solution.py:46
  444.4 10.5 %collective-permute-start.5 = (bf16[128,3584]{1,0:T(8,128)(2,1)S(1)}, bf16[128,3584]{1,0:T(8,128)(2,1)S(1)}, u32[]{:S(2)}, u32[]{:S(2)}) collective-permute-start(bf16[128,3584]{1,0:T(8,128)(2,1)S(1)} %copy-done.3), channel_id=1, source_target_pairs={{0,4},{4,0},{1,5},{5,1},{2,6},{6,2},{3,7},{7,3},{8,12},{12,8},{9,1... | collective-permute-start | bytes 2752520 | tf_op jit(solution)/shard_map/ppermute | solution.py:46
  506.1 14.1 %all-to-all-start.2 = ((bf16[16,64,128]{2,1,0:T(8,128)(2,1)}), bf16[16,64,128]{2,1,0:T(8,128)(2,1)}, u32[]{:S(2)}, u32[]{:S(2)}) async-start(bf16[16,64,128]{2,1,0:T(8,128)(2,1)} %bitcast.9), calls=%async_computation.2 | async-start | bytes 524288 | tf_op jit(solution)/shard_map/all_to_all | solution.py:129
  520.2 15.8 %all-to-all-start.5 = ((bf16[4,64,512]{2,1,0:T(8,128)(2,1)}), bf16[4,64,512]{2,1,0:T(8,128)(2,1)}, u32[]{:S(2)}, u32[]{:S(2)}) async-start(bf16[4,64,512]{2,1,0:T(8,128)(2,1)} %bitcast.74), calls=%async_computation.5 | async-start | bytes 524288 | tf_op jit(solution)/shard_map/all_to_all | solution.py:167
  524.4 25.8 %copy-start.1 = (bf16[6400,256]{1,0:T(8,128)(2,1)S(1)}, bf16[6400,256]{1,0:T(8,128)(2,1)}, u32[]{:S(2)}) copy-start(bf16[6400,256]{1,0:T(8,128)(2,1)} %param.18) | copy-start | bytes 9830404
  536.0 13.5 %all-to-all-start.6 = ((bf16[4,64,512]{2,1,0:T(8,128)(2,1)}), bf16[4,64,512]{2,1,0:T(8,128)(2,1)S(1)}, u32[]{:S(2)}, u32[]{:S(2)}) async-start(bf16[4,64,512]{2,1,0:T(8,128)(2,1)} %select_select_fusion), calls=%async_computation.6 | async-start | bytes 524288 | tf_op jit(solution)/shard_map/all_to_all | solution.py:166
Sparse Core Ops, SparseCore 0:
  17.9 178.5 all-gather.8
  198.0 8.4 all-gather.12
  211.2 86.9 all-gather.10
  299.7 26.1 all-gather.18
  327.8 27.4 all-gather.16
  356.7 27.4 all-gather.14
  505.4 27.0 all-gather.20

commit v2 on v1

--- a/solution.py
+++ b/solution.py
@@ -3,6 +3,8 @@
 import jax
 import jax.numpy as jnp
 from jax import lax
+from jax.experimental import pallas as pl
+from jax.experimental.pallas import tpu as pltpu
 from jax.sharding import PartitionSpec as P
 
 TOK_DEV = 128
@@ -40,6 +42,148 @@
     gate_grad = (hidden_grad * up * sig * (1.0 + gate * (1.0 - sig))).astype(jnp.bfloat16)
     up_grad = (hidden_grad * gate * sig).astype(jnp.bfloat16)
     return (gate_grad, up_grad)
+
+
+def gather_kernel(groups, mps, x_ref, out_ref, local_sem, send_sem, recv_sem):
+    g, m = lax.axis_index("group"), lax.axis_index("mp")
+    gx = g + 1 - 2 * (g % 2)
+    gy = g + 2 - 4 * (g // 2)
+    gd = 3 - g
+    rows, width = x_ref.shape
+    cut, half = rows - rows // 4, width // 2
+    head, tail = pl.ds(0, cut), pl.ds(cut, rows - cut)
+    every, left, right = pl.ds(0, width), pl.ds(0, half), pl.ds(half, width - half)
+    slots, sent = {}, []
+    to_x, to_y = {"group": gx}, {"group": gy}
+    low, high = {"mp": m - 1}, {"mp": m + 1}
+
+    def slot(key):
+        return slots.setdefault(key, len(slots))
+
+    def send(key, owner, line, part, cols, target, when=None, own=False):
+        dst = out_ref.at[owner, line, part, cols]
+        copy = pltpu.make_async_remote_copy(
+            src_ref=x_ref.at[part, cols] if own else dst,
+            dst_ref=dst,
+            send_sem=send_sem.at[slot(key)],
+            recv_sem=recv_sem.at[slot(key)],
+            device_id=target,
+            device_id_type=pl.DeviceIdType.MESH,
+        )
+        guarded(when, copy.start)
+        sent.append((when, copy))
+
+    def arrive(key, owner, line, part, cols, source, when=None):
+        dst = out_ref.at[owner, line, part, cols]
+        copy = pltpu.make_async_remote_copy(
+            src_ref=dst,
+            dst_ref=dst,
+            send_sem=send_sem.at[slot(key)],
+            recv_sem=recv_sem.at[slot(key)],
+            device_id=source,
+            device_id_type=pl.DeviceIdType.MESH,
+        )
+        guarded(when, copy.wait_recv)
+
+    def guarded(when, act):
+        if when is None:
+            act()
+        else:
+            pl.when(when)(lambda: act())
+
+    barrier = pltpu.get_barrier_semaphore()
+    has_low, has_high = m > 0, m < mps - 1
+
+    def greet(target):
+        pl.semaphore_signal(
+            barrier, inc=1, device_id=target, device_id_type=pl.DeviceIdType.MESH
+        )
+
+    greet(to_x)
+    greet(to_y)
+    guarded(has_low, lambda: greet(low))
+    guarded(has_high, lambda: greet(high))
+    pl.semaphore_wait(barrier, 2 + (m + mps - 1) // mps + (2 * mps - 2 - m) // mps)
+
+    keep = pltpu.make_async_copy(x_ref, out_ref.at[g, m], local_sem)
+    keep.start()
+    send(("up", 0), g, m, head, every, high, has_high, True)
+    send(("down", 0), g, m, head, every, low, has_low, True)
+    send("tail_x", g, m, tail, every, to_x, None, True)
+    send("tail_y", g, m, tail, every, to_y, None, True)
+    send(("x", 0, 0), g, m, head, every, to_x, None, True)
+    send(("y", 0, 0), g, m, head, every, to_y, None, True)
+    send(("up", 0, 0), g, m, tail, every, high, has_high, True)
+    send(("down", 0, 0), g, m, tail, every, low, has_low, True)
+
+    arrive("tail_x", gx, m, tail, every, to_x)
+    send("tail_xy", gx, m, tail, left, to_y)
+    arrive("tail_y", gy, m, tail, every, to_y)
+    send("tail_yx", gy, m, tail, right, to_x)
+    for owner, j in ((gx, 1), (gy, 2)):
+        send(("up", 0, j), owner, m, tail, every, high, has_high)
+        send(("down", 0, j), owner, m, tail, every, low, has_low)
+    arrive("tail_xy", gd, m, tail, left, to_y)
+    arrive("tail_yx", gd, m, tail, right, to_x)
+    send(("up", 0, 3), gd, m, tail, every, high, has_high)
+    send(("down", 0, 3), gd, m, tail, every, low, has_low)
+
+    def turn(key, line, when=None):
+        arrive(("x",) + key, gx, line, head, every, to_x, when)
+        send(("xy",) + key, gx, line, head, left, to_y, when)
+        arrive(("y",) + key, gy, line, head, every, to_y, when)
+        send(("yx",) + key, gy, line, head, right, to_x, when)
+
+    turn((0, 0), m)
+    lines = [((0, 0), m, None)]
+    for step in range(1, mps):
+        ways = (
+            ("up", m - step, m >= step, low, high, (m >= step) & has_high),
+            ("down", m + step, m < mps - step, high, low, (m < mps - step) & has_low),
+        )
+        for name, line, come, source, target, on in ways:
+            arrive((name, step - 1), g, line, head, every, source, come)
+            if step < mps - 1:
+                send((name, step), g, line, head, every, target, on)
+            send(("x", name, step), g, line, head, every, to_x, come)
+            send(("y", name, step), g, line, head, every, to_y, come)
+        for name, line, come, source, target, on in ways:
+            for owner, j in ((g, 0), (gx, 1), (gy, 2), (gd, 3)):
+                arrive((name, step - 1, j), owner, line, tail, every, source, come)
+                if step < mps - 1:
+                    send((name, step, j), owner, line, tail, every, target, on)
+        for name, line, come, source, target, on in ways:
+            turn((name, step), line, come)
+            lines.append(((name, step), line, come))
+    for key, line, come in lines:
+        arrive(("xy",) + key, gd, line, head, left, to_y, come)
+        arrive(("yx",) + key, gd, line, head, right, to_x, come)
+    for when, copy in sent:
+        guarded(when, copy.wait_send)
+    keep.wait()
+
+
+def gather_blocks(value, groups, mps, ident):
+    rows, width = value.shape
+    if groups != 4 or mps < 2 or rows % 64 or width % 256:
+        whole = lax.all_gather(value, ("group", "mp"), axis=0, tiled=False)
+        return whole.reshape(groups, mps, rows, width)
+    count = 4 + 2 * (mps - 1) * 5 + 4 * (2 * mps - 1)
+    return pl.pallas_call(
+        functools.partial(gather_kernel, groups, mps),
+        out_shape=jax.ShapeDtypeStruct((groups, mps, rows, width), value.dtype),
+        in_specs=[pl.BlockSpec(memory_space=pl.ANY)],
+        out_specs=pl.BlockSpec(memory_space=pl.ANY),
+        scratch_shapes=[
+            pltpu.SemaphoreType.DMA(()),
+            pltpu.SemaphoreType.DMA((count,)),
+            pltpu.SemaphoreType.DMA((count,)),
+        ],
+        compiler_params=pltpu.CompilerParams(collective_id=ident, has_side_effects=True),
+        cost_estimate=pl.CostEstimate(
+            flops=0, bytes_accessed=2 * groups * mps * rows * width * 2, transcendentals=0
+        ),
+    )(value)
 
 
 def swap_dp(value):
@@ -94,7 +238,7 @@
     centred = values - mean[:, None]
     spread = lax.psum(jnp.sum(centred * centred, axis=1), "dp") / (patches.shape[1] * dps)
     normed = (centred * lax.rsqrt(spread + 1e-05)[:, None] * norm_gain + norm_bias).astype(bf16)
-    normed_all = lax.all_gather(normed, ("group", "mp"), axis=0, tiled=True)
+    normed_all = gather_blocks(normed, groups, mps, 0).reshape(total, -1)
 
     def matmul(a, b):
         return jnp.dot(a, b, preferred_element_type=f32)
@@ -112,7 +256,8 @@
 
     first = summed_share(normed_all, lambda rows: matmul(rows, proj_in))
     activated = jax.nn.gelu(first + proj_in_bias, approximate=False).astype(bf16)
-    activated_all = lax.all_gather(activated, rank, axis=1, tiled=True)
+    activated_all = gather_blocks(activated, groups, mps, 1).transpose(2, 1, 0, 3)
+    activated_all = activated_all.reshape(activated.shape[0], -1)
     columns = (matmul(activated_all, out_cols) + out_bias).astype(bf16)
     columns = lax.all_to_all(columns, "dp", 1, 0, tiled=True)
 

time: 558 us -> 485 us (0.87); the launches traced: 557 us -> 476 us
  waiting for transfers between devices: 284 us -> 84.3 us
  Pallas kernels: 0 us -> 156 us
  blocking collectives: 102 us -> 48.5 us
  starting transfers between devices: 15 us -> 23.2 us
  local copies, waits for them, and re-layouts: 17.3 us -> 24.7 us
    all_gather x2 -> x0, waiting for transfers between devices: 205 us -> none  [the longest x1 122 us: local(): normed_all = lax.all_gather(normed, ('group', 'mp'), axis=0, tiled=True)]
    pallas_call x0 -> x2, Pallas kernels: none -> 156 us  [gather_blocks(): pl.pallas_call(functools.partial(gather_kernel, groups, mps), out_shape=j...]
    all_to_all x1 -> x0, blocking collectives: 52.5 us -> none  [local(): out_cols = lax.all_to_all(proj_out, rank, 1, 0, tiled=True)]
    all_to_all x0 -> x1, waiting for transfers between devices: none -> 16.6 us  [local(): out_cols = lax.all_to_all(proj_out, rank, 1, 0, tiled=True)]
    all_to_all x0 -> x1, starting transfers between devices: none -> 8.36 us  [local(): out_cols = lax.all_to_all(proj_out, rank, 1, 0, tiled=True)]
    transpose x0 -> x1, local copies, waits for them, and re-layouts: none -> 7.3 us  [local(): gather_blocks(activated, groups, mps, 1).transpose(2, 1, 0, 3)]
  transfers between devices with their start and end apart: 16 -> 15, of which waited for: 9 -> 6; matrix products, arithmetic and copies ran while one was open for 19% -> 24% of each run, Pallas kernels for 0% -> 33%
where the time goes in v2:
time: 485 us; the launch traced here: 476 us
  Pallas kernels  156 us (32%)
  matrix products  114 us (24%)
  waiting for transfers between devices  84.3 us (17%)
  blocking collectives  48.5 us (10%)
  local copies, waits for them, and re-layouts  24.7 us (5%)
  starting transfers between devices  23.2 us (5%)
  between operations  14.6 us (3%)
  other arithmetic  10 us (2%)
    pallas_call x2, Pallas kernels, gather_blocks(): pl.pallas_call(functools.partial(gather_kernel, groups, mps), out_shape=j...  156 us
    dot_general x6, matrix products, matmul_t(): lax.dot_general(a, b, (((1,), (1,)), ((), ())), preferred_element_type=f32)  64.8 us
    dot_general x7, matrix products, matmul(): return jnp.dot(a, b, preferred_element_type=f32)  49.5 us
    all_to_all x1, blocking collectives, local(): lax.all_to_all(partial.reshape(group_rows, mps, share).swapaxes(0, 1), 'm...  29 us
    all_gather x1, waiting for transfers between devices, local(): placed = lax.all_gather(placed, 'mp', axis=1, tiled=True)  25.6 us
    all_gather x1, waiting for transfers between devices, local(): lax.all_gather(out_grads, 'mp', axis=0, tiled=True)  18.6 us
    all_to_all x1, waiting for transfers between devices, local(): out_cols = lax.all_to_all(proj_out, rank, 1, 0, tiled=True)  16.6 us
  transfers between devices with their start and end apart: 15, of which 6 were waited for; matrix products, arithmetic and copies ran while one was open for 24% of the time, Pallas kernels for 33%

profile of v2, /device:TPU:0, one launch (start us, length us, event | category | flops | bytes accessed | tf_op | source)
XLA Modules:
  0.0 476.0 jit_solution(7369901434171326493)
XLA Ops:
  7.2 2.4 copy.63
  9.6 8.4 %all-to-all-start = ((bf16[256,16,128]{0,2,1:T(8,128)(2,1)}), bf16[256,16,128]{0,2,1:T(8,128)(2,1)}, u32[]{:S(2)}, u32[]{:S(2)}) async-start(bf16[256,16,128]{0,2,1:T(8,128)(2,1)} %bitcast.79), calls=%async_computation | async-start | bytes 2097152 | tf_op jit(solution)/shard_map/all_to_all | solution.py:226
  18.0 1.4 convert_reduce_fusion
  19.4 2.5 psum.14
  21.9 1.5 fusion.12
  23.4 2.5 psum.15
  25.9 16.6 %all-to-all-done = bf16[256,16,128]{0,2,1:T(8,128)(2,1)} async-done(((bf16[256,16,128]{0,2,1:T(8,128)(2,1)}), bf16[256,16,128]{0,2,1:T(8,128)(2,1)}, u32[]{:S(2)}, u32[]{:S(2)}) %all-to-all-start) | async-done | bytes 1048608 | tf_op jit(solution)/shard_map/all_to_all | solution.py:226
  42.5 2.3 copy.64
  44.8 2.4 fusion.15.x_ref
  47.2 103.4 %shard_map.166 = bf16[4,4,64,6400]{3,2,1,0:T(8,128)(2,1)} custom-call(bf16[64,6400]{1,0:T(8,128)(2,1)} %fusion.15.x_ref), custom_call_target="tpu_custom_call" | custom-call | bytes 26214400 | tf_op jit(solution)/shard_map/pallas_call | solution.py:172
  150.7 5.5 %fusion = f32[512,256]{1,0:T(8,128)} fusion(bf16[6400,256]{1,0:T(8,128)(2,1)S(1)} %copy-done, bf16[1024,6400]{1,0:T(8,128)(2,1)} %bitcast.75, s32[]{:T(128)S(6)} %select_n.116), kind=kOutput, calls=%fused_computation.2 | convolution fusion | flops 1677721600 | bytes 10354692 | tf_op jit(solution)/shard_map/dot_general | solution.py:244
  156.7 0.8 dynamic-slice_bitcast_fusion
  157.5 2.0 all-gather
  159.5 6.6 %fusion.26.x_ref = bf16[512,256]{1,0:T(8,128)(2,1)} fusion(f32[512,256]{1,0:T(8,128)} %collective-permute-done, bf16[6400,256]{1,0:T(8,128)(2,1)S(1)} %copy-done, bf16[1024,6400]{1,0:T(8,128)(2,1)} %bitcast.76, s32[]{:T(128)S(6)} %select_n.115, f32[256]{0:T(256)S(1)} %copy-done.9), kind=kOutput, calls=%fused_computation.37 | convolution fusion | flops 1686503424 | bytes 10617860 | tf_op jit(solution)/shard_map/dot_general | solution.py:244
  166.1 53.1 %shard_map.167 = bf16[4,4,512,256]{3,2,1,0:T(8,128)(2,1)} custom-call(bf16[512,256]{1,0:T(8,128)(2,1)} %fusion.26.x_ref), custom_call_target="tpu_custom_call" | custom-call | bytes 8388608 | tf_op jit(solution)/shard_map/pallas_call | solution.py:172
  219.1 7.3 %copy.62 = bf16[512,4,4,256]{0,3,2,1:T(8,128)(2,1)} copy(bf16[512,4,4,256]{3,0,1,2:T(8,128)(2,1)} %bitcast.74) | data formatting | bytes 8388608 | tf_op jit(solution)/shard_map/transpose | solution.py:259
  226.4 4.2 fusion.22
  230.8 3.9 all_to_all.113
  234.7 3.2 gather_fusion
  238.1 8.7 %all_to_all.114 = bf16[4,256,128]{2,1,0:T(8,128)(2,1)S(1)} all-to-all(bf16[4,256,128]{2,1,0:T(8,128)(2,1)S(1)} %broadcast_select_fusion.1), channel_id=1, replica_groups=mesh['group'=4,'dp'=2,'mp'=4] {'group'}, dimensions={0} | all-to-all | bytes 524288 | tf_op jit(solution)/shard_map/all_to_all | solution.py:268
  246.8 0.7 copy_bitcast_fusion.2
  248.6 25.6 %all-gather.11.cloned.1.call-done = bf16[256,2048]{1,0:T(8,128)(2,1)} async-done(((bf16[256,512]{1,0:T(8,128)(2,1)}), bf16[256,2048]{1,0:T(8,128)(2,1)}) %all-gather.11.cloned.1.call-update) | async-done | bytes 1048592 | tf_op jit(solution)/shard_map/all_gather | solution.py:269
  274.2 1.7 broadcast_select_fusion
  275.9 8.5 %fusion.39 = f32[128,3584]{1,0:T(8,128)} fusion(bf16[2048,3584]{1,0:T(8,128)(2,1)} %param.24, bf16[256,2048]{1,0:T(8,128)(2,1)S(1)} %broadcast_select_fusion, s32[]{:T(128)S(6)} %select_n.120), kind=kOutput, calls=%fused_computation.58 | convolution fusion | flops 1879048192 | bytes 17039364 | tf_op jit(solution)/shard_map/dot_general | solution.py:244
  284.4 18.6 %all-gather.9.cloned.1.call-done = bf16[256,2048]{1,0:T(8,128)(2,1)} async-done(((bf16[64,2048]{1,0:T(8,128)(2,1)}), bf16[256,2048]{1,0:T(8,128)(2,1)}) %all-gather.9.cloned.1.call-update) | async-done | bytes 1048592 | tf_op jit(solution)/shard_map/all_gather | solution.py:233
  303.0 11.5 %fusion.27 = f32[128,3584]{1,0:T(8,128)} fusion(bf16[3584,2048]{1,0:T(8,128)(2,1)} %param.26, bf16[256,2048]{1,0:T(8,128)(2,1)} %all-gather.9.cloned.1.call-done, s32[]{:T(128)S(6)} %select_n.120), kind=kOutput, calls=%fused_computation.40 | convolution fusion | flops 1879048192 | bytes 17039364 | tf_op jit(solution)/shard_map/dot_general | solution.py:247
  314.6 7.2 %fusion.41 = f32[128,3584]{1,0:T(8,128)S(1)} fusion(bf16[2048,3584]{1,0:T(8,128)(2,1)} %param.25, bf16[256,2048]{1,0:T(8,128)(2,1)S(1)} %broadcast_select_fusion, s32[]{:T(128)S(6)} %select_n.120), kind=kOutput, calls=%fused_computation.60 | convolution fusion | flops 1879048192 | bytes 17039364 | tf_op jit(solution)/shard_map/dot_general | solution.py:244
  322.4 8.5 %convolution_add_fusion = f32[128,3584]{1,0:T(8,128)} fusion(f32[128,3584]{1,0:T(8,128)S(1)} %collective-permute-done.3, bf16[2048,3584]{1,0:T(8,128)(2,1)} %param.24, bf16[256,2048]{1,0:T(8,128)(2,1)S(1)} %broadcast_select_fusion, s32[]{:T(128)S(6)} %select_n.119), kind=kOutput, calls=%fused_computation.6 | convolution fusion | flops 1879506944 | bytes 18874372 | tf_op jit(solution)/shard_map/dot_general | solution.py:244
  330.9 13.3 %multiply_convert_fusion = (bf16[128,3584]{1,0:T(8,128)(2,1)}, f32[128,3584]{1,0:T(8,128)}) fusion(f32[128,3584]{1,0:T(8,128)} %convolution_add_fusion, f32[128,3584]{1,0:T(8,128)} %collective-permute-done.1, bf16[3584,2048]{1,0:T(8,128)(2,1)} %param.26, bf16[256,2048]{1,0:T(8,128)(2,1)} %all-gather.9.cloned.1.call-done, s32[]{:T(128)S(6)} %select_n.119), kind=kOutput, calls=%fused_computation.21 | convolution fusion | flops 1882259456 | bytes 21626884 | tf_op jit(solution)/shard_map/dot_general | solution.py:247
  344.2 8.9 %fusion.7 = bf16[128,3584]{1,0:T(8,128)(2,1)S(1)} fusion(f32[128,3584]{1,0:T(8,128)} %get-tuple-element.7, f32[128,3584]{1,0:T(8,128)} %collective-permute-done.2, bf16[2048,3584]{1,0:T(8,128)(2,1)} %param.25, f32[128,3584]{1,0:T(8,128)S(1)} %copy-done.2, bf16[256,2048]{1,0:T(8,128)(2,1)S(1)} %broadcast_select_fusion, s32[]{:T(128)S(6)} %select_n.119), kind=kOutput, calls=%fused_computation.12 | convolution fusion | flops 1884094464 | bytes 21626884 | tf_op jit(solution)/shard_map/dot_general | solution.py:244
  353.1 10.0 %fusion.62 = f32[128,2048]{1,0:T(8,128)S(1)} fusion(bf16[128,3584]{1,0:T(8,128)(2,1)S(1)} %fusion.7, bf16[2048,3584]{1,0:T(8,128)(2,1)} %param.24), kind=kOutput, calls=%fused_computation.106 | convolution fusion | flops 1879048192 | bytes 16646144 | tf_op jit(solution)/shard_map/dot_general | solution.py:247
  363.7 9.9 %fusion.8 = bf16[128,2048]{1,0:T(8,128)(2,1)S(1)} fusion(f32[128,2048]{1,0:T(8,128)S(1)} %fusion.62, bf16[128,3584]{1,0:T(8,128)(2,1)S(1)} %copy-done.3, bf16[2048,3584]{1,0:T(8,128)(2,1)} %param.25), kind=kOutput, calls=%fused_computation.15 | convolution fusion | flops 1879572480 | bytes 17170432 | tf_op jit(solution)/shard_map/dot_general | solution.py:247
  373.7 9.9 %fusion.63 = f32[128,2048]{1,0:T(8,128)S(1)} fusion(bf16[128,3584]{1,0:T(8,128)(2,1)S(1)} %collective-permute-done.5, bf16[2048,3584]{1,0:T(8,128)(2,1)} %param.25), kind=kOutput, calls=%fused_computation.107 | convolution fusion | flops 1879048192 | bytes 16646144 | tf_op jit(solution)/shard_map/dot_general | solution.py:247
  383.6 10.2 %fusion.9 = bf16[128,2048]{1,0:T(8,128)(2,1)S(1)} fusion(f32[128,2048]{1,0:T(8,128)S(1)} %fusion.63, bf16[128,3584]{1,0:T(8,128)(2,1)S(1)} %collective-permute-done.4, bf16[2048,3584]{1,0:T(8,128)(2,1)} %param.24), kind=kOutput, calls=%fused_computation.16 | convolution fusion | flops 1879572480 | bytes 17170432 | tf_op jit(solution)/shard_map/dot_general | solution.py:247
  394.3 29.0 %all_to_all.115 = bf16[4,256,512]{2,1,0:T(8,128)(2,1)S(1)} all-to-all(bf16[4,256,512]{2,1,0:T(8,128)(2,1)S(1)} %fusion.23), channel_id=1, replica_groups=mesh['group'=4,'dp'=2,'mp'=4] {'mp'}, dimensions={0} | all-to-all | bytes 2097152 | tf_op jit(solution)/shard_map/all_to_all | solution.py:296
  423.2 0.9 reduce_sum.61
  424.2 0.7 copy.66
  424.9 4.7 all-to-all-start.2
  429.8 9.2 %all-to-all-done.2 = bf16[16,64,128]{2,1,0:T(8,128)(2,1)} async-done(((bf16[16,64,128]{2,1,0:T(8,128)(2,1)}), bf16[16,64,128]{2,1,0:T(8,128)(2,1)}, u32[]{:S(2)}, u32[]{:S(2)}) %all-to-all-start.2) | async-done | bytes 262176 | tf_op jit(solution)/shard_map/all_to_all | solution.py:274
  439.0 4.0 all-to-all-start.5
  443.3 8.1 %all-gather.15.cloned.1.call-done = bf16[1024,512]{1,0:T(8,128)(2,1)} async-done(((bf16[256,512]{1,0:T(8,128)(2,1)}), bf16[1024,512]{1,0:T(8,128)(2,1)}) %all-gather.15.cloned.1.call-update) | async-done | bytes 1048592 | tf_op jit(solution)/shard_map/all_gather | solution.py:301
  451.4 2.6 gather_fusion.1
  454.0 0.8 select_select_fusion
  454.8 4.6 all-to-all-start.6
  459.4 1.7 copy_bitcast_fusion.3
  461.1 1.7 copy.80
  462.8 5.6 %all-to-all-done.6 = bf16[4,64,512]{2,1,0:T(8,128)(2,1)S(1)} async-done(((bf16[4,64,512]{2,1,0:T(8,128)(2,1)}), bf16[4,64,512]{2,1,0:T(8,128)(2,1)S(1)}, u32[]{:S(2)}, u32[]{:S(2)}) %all-to-all-start.6) | async-done | bytes 262176 | tf_op jit(solution)/shard_map/all_to_all | solution.py:311
  468.3 0.7 copy.81
  (72 shorter events, 4.1 us)
Async XLA Ops:
  7.2 143.4 %copy-start = (bf16[6400,256]{1,0:T(8,128)(2,1)S(1)}, bf16[6400,256]{1,0:T(8,128)(2,1)}, u32[]{:S(2)}) copy-start(bf16[6400,256]{1,0:T(8,128)(2,1)} %param.18) | copy-start | bytes 9830404
  9.6 32.9 %all-to-all-start = ((bf16[256,16,128]{0,2,1:T(8,128)(2,1)}), bf16[256,16,128]{0,2,1:T(8,128)(2,1)}, u32[]{:S(2)}, u32[]{:S(2)}) async-start(bf16[256,16,128]{0,2,1:T(8,128)(2,1)} %bitcast.79), calls=%async_computation | async-start | bytes 2097152 | tf_op jit(solution)/shard_map/all_to_all | solution.py:226
  18.0 208.4 %all-gather.7.cloned.1.call-start = ((), (), s32[]{:S(2)}) async-start(), calls=%async_computation.7 | async-start | bytes 3145728 | tf_op jit(solution)/shard_map/all_gather | solution.py:227
  19.4 25.4 %copy-start.4 = (f32[6400]{0:T(1024)S(1)}, f32[6400]{0:T(1024)}, u32[]{:S(2)}) copy-start(f32[6400]{0:T(1024)} %param.17) | copy-start | bytes 76804
  19.4 25.4 %copy-start.5 = (f32[6400]{0:T(1024)S(1)}, f32[6400]{0:T(1024)}, u32[]{:S(2)}) copy-start(f32[6400]{0:T(1024)} %param.16) | copy-start | bytes 76804
  44.8 203.8 %all-gather.13.cloned.1.call-start = ((), (), s32[]{:S(2)}) async-start(), calls=%async_computation.10 | async-start | bytes 1310720 | tf_op jit(solution)/shard_map/all_gather | solution.py:232
  150.6 5.7 %copy-start.8 = (s32[16]{0:T(128)S(1)}, s32[16]{0:T(128)}, u32[]{:S(2)}) copy-start(s32[16]{0:T(128)} %param.27) | copy-start | bytes 196
  150.6 5.9 %copy-start.6 = (s32[16]{0:T(128)S(1)}, s32[16]{0:T(128)}, u32[]{:S(2)}) copy-start(s32[16]{0:T(128)} %param.29) | copy-start | bytes 196
  150.6 5.9 %copy-start.7 = (s32[16]{0:T(128)S(1)}, s32[16]{0:T(128)}, u32[]{:S(2)}) copy-start(s32[16]{0:T(128)} %param.28) | copy-start | bytes 196
  150.7 8.8 %copy-start.9 = (f32[256]{0:T(256)S(1)}, f32[256]{0:T(256)}, u32[]{:S(2)}) copy-start(f32[256]{0:T(256)} %param.19) | copy-start | bytes 3076
  156.2 3.2 collective-permute-start
  156.2 117.9 %all-gather.11.cloned.1.call-start = ((), (), s32[]{:S(2)}) async-start(), calls=%async_computation.9 | async-start | bytes 1310720 | tf_op jit(solution)/shard_map/all_gather | solution.py:269
  247.6 55.5 %all-gather.9.cloned.1.call-start = ((), (), s32[]{:S(2)}) async-start(), calls=%async_computation.8 | async-start | bytes 1310720 | tf_op jit(solution)/shard_map/all_gather | solution.py:233
  248.2 203.2 %all-gather.15.cloned.1.call-start = ((), (), s32[]{:S(2)}) async-start(), calls=%async_computation.11 | async-start | bytes 1310720 | tf_op jit(solution)/shard_map/all_gather | solution.py:301
  284.4 38.0 %collective-permute-start.3 = (f32[128,3584]{1,0:T(8,128)}, f32[128,3584]{1,0:T(8,128)S(1)}, u32[]{:S(2)}, u32[]{:S(2)}) collective-permute-start(f32[128,3584]{1,0:T(8,128)} %fusion.39), channel_id=1, source_target_pairs={{0,4},{4,0},{1,5},{5,1},{2,6},{6,2},{3,7},{7,3},{8,12},{12,8},{9,1... | collective-permute-start | bytes 5505032 | tf_op jit(solution)/shard_map/ppermute | solution.py:190
  314.6 16.4 %collective-permute-start.1 = (f32[128,3584]{1,0:T(8,128)}, f32[128,3584]{1,0:T(8,128)}, u32[]{:S(2)}, u32[]{:S(2)}) collective-permute-start(f32[128,3584]{1,0:T(8,128)} %fusion.27), channel_id=1, source_target_pairs={{0,4},{4,0},{1,5},{5,1},{2,6},{6,2},{3,7},{7,3},{8,12},{12,8},{9,1... | collective-permute-start | bytes 5505032 | tf_op jit(solution)/shard_map/ppermute | solution.py:190
  321.8 22.4 %collective-permute-start.2 = (f32[128,3584]{1,0:T(8,128)S(1)}, f32[128,3584]{1,0:T(8,128)}, u32[]{:S(2)}, u32[]{:S(2)}) collective-permute-start(f32[128,3584]{1,0:T(8,128)S(1)} %fusion.41), channel_id=1, source_target_pairs={{0,4},{4,0},{1,5},{5,1},{2,6},{6,2},{3,7},{7,3},{8,12},{12,8},{9,1... | collective-permute-start | bytes 5505032 | tf_op jit(solution)/shard_map/ppermute | solution.py:190
  330.9 13.3 %copy-start.2 = (f32[128,3584]{1,0:T(8,128)S(1)}, f32[128,3584]{1,0:T(8,128)}, u32[]{:S(2)}) copy-start(f32[128,3584]{1,0:T(8,128)} %convolution_add_fusion) | copy-start | bytes 5505028
  353.1 10.1 %copy-start.3 = (bf16[128,3584]{1,0:T(8,128)(2,1)S(1)}, bf16[128,3584]{1,0:T(8,128)(2,1)}, u32[]{:S(2)}) copy-start(bf16[128,3584]{1,0:T(8,128)(2,1)} %get-tuple-element.6) | copy-start | bytes 2752516
  363.1 20.5 %collective-permute-start.4 = (bf16[128,3584]{1,0:T(8,128)(2,1)S(1)}, bf16[128,3584]{1,0:T(8,128)(2,1)S(1)}, u32[]{:S(2)}, u32[]{:S(2)}) collective-permute-start(bf16[128,3584]{1,0:T(8,128)(2,1)S(1)} %fusion.7), channel_id=1, source_target_pairs={{0,4},{4,0},{1,5},{5,1},{2,6},{6,2},{3,7},{7,3},{8,12},{12,8},{9,1... | collective-permute-start | bytes 2752520 | tf_op jit(solution)/shard_map/ppermute | solution.py:190
  363.2 10.5 %collective-permute-start.5 = (bf16[128,3584]{1,0:T(8,128)(2,1)S(1)}, bf16[128,3584]{1,0:T(8,128)(2,1)S(1)}, u32[]{:S(2)}, u32[]{:S(2)}) collective-permute-start(bf16[128,3584]{1,0:T(8,128)(2,1)S(1)} %copy-done.3), channel_id=1, source_target_pairs={{0,4},{4,0},{1,5},{5,1},{2,6},{6,2},{3,7},{7,3},{8,12},{12,8},{9,1... | collective-permute-start | bytes 2752520 | tf_op jit(solution)/shard_map/ppermute | solution.py:190
  424.9 14.1 %all-to-all-start.2 = ((bf16[16,64,128]{2,1,0:T(8,128)(2,1)}), bf16[16,64,128]{2,1,0:T(8,128)(2,1)}, u32[]{:S(2)}, u32[]{:S(2)}) async-start(bf16[16,64,128]{2,1,0:T(8,128)(2,1)} %bitcast.12), calls=%async_computation.2 | async-start | bytes 524288 | tf_op jit(solution)/shard_map/all_to_all | solution.py:274
  439.0 15.8 %all-to-all-start.5 = ((bf16[4,64,512]{2,1,0:T(8,128)(2,1)}), bf16[4,64,512]{2,1,0:T(8,128)(2,1)}, u32[]{:S(2)}, u32[]{:S(2)}) async-start(bf16[4,64,512]{2,1,0:T(8,128)(2,1)} %bitcast.80), calls=%async_computation.5 | async-start | bytes 524288 | tf_op jit(solution)/shard_map/all_to_all | solution.py:312
  443.3 25.8 %copy-start.1 = (bf16[6400,256]{1,0:T(8,128)(2,1)S(1)}, bf16[6400,256]{1,0:T(8,128)(2,1)}, u32[]{:S(2)}) copy-start(bf16[6400,256]{1,0:T(8,128)(2,1)} %param.18) | copy-start | bytes 9830404
  454.8 13.5 %all-to-all-start.6 = ((bf16[4,64,512]{2,1,0:T(8,128)(2,1)}), bf16[4,64,512]{2,1,0:T(8,128)(2,1)S(1)}, u32[]{:S(2)}, u32[]{:S(2)}) async-start(bf16[4,64,512]{2,1,0:T(8,128)(2,1)} %select_select_fusion), calls=%async_computation.6 | async-start | bytes 524288 | tf_op jit(solution)/shard_map/all_to_all | solution.py:311
Sparse Core Ops, SparseCore 0:
  44.9 10.5 all-gather.6
  156.4 36.7 all-gather.12
  247.7 26.4 all-gather.10
  275.6 27.4 all-gather.8
  424.3 27.0 all-gather.14

commit v3 on v2

--- a/solution.py
+++ b/solution.py
@@ -252,12 +252,14 @@
             return op(half_rows(value, dp)) + arriving
         return lax.psum_scatter(op(value), "dp", scatter_dimension=0, tiled=True)
 
-    hidden_grad = summed_share(seq_cotangent, lambda rows: matmul_t(rows, down_weight))
-
     first = summed_share(normed_all, lambda rows: matmul(rows, proj_in))
     activated = jax.nn.gelu(first + proj_in_bias, approximate=False).astype(bf16)
+    activated, seq_text, seq_cotangent = lax.optimization_barrier(
+        (activated, seq_text, seq_cotangent)
+    )
     activated_all = gather_blocks(activated, groups, mps, 1).transpose(2, 1, 0, 3)
     activated_all = activated_all.reshape(activated.shape[0], -1)
+    hidden_grad = summed_share(seq_cotangent, lambda rows: matmul_t(rows, down_weight))
     columns = (matmul(activated_all, out_cols) + out_bias).astype(bf16)
     columns = lax.all_to_all(columns, "dp", 1, 0, tiled=True)
 

time: 485 us -> 479 us (0.988)
  waiting for transfers between devices: 84.3 us -> 50.7 us
  Pallas kernels: 156 us -> 185 us
    pallas_call x2, Pallas kernels: 156 us -> 185 us  [gather_blocks(): pl.pallas_call(functools.partial(gather_kernel, groups, mps), out_shape=j...]
    all_gather x1, waiting for transfers between devices: 18.6 us -> 0.01 us  [local(): lax.all_gather(out_grads, 'mp', axis=0, tiled=True)]
    all_to_all x1, waiting for transfers between devices: 16.6 us -> 0.01 us  [local(): out_cols = lax.all_to_all(proj_out, rank, 1, 0, tiled=True)]
  transfers between devices with their start and end apart: 15 -> 15, of which waited for: 6 -> 4; matrix products, arithmetic and copies ran while one was open for 24% -> 21% of each run, Pallas kernels for 33% -> 39%
where the time goes in v3:
time: 479 us; the launch traced here: 471 us
  Pallas kernels  185 us (39%)
  matrix products  114 us (24%)
  waiting for transfers between devices  50.7 us (11%)
  blocking collectives  48.9 us (10%)
  local copies, waits for them, and re-layouts  24.8 us (5%)
  starting transfers between devices  23.4 us (5%)
  between operations  14.6 us (3%)
  other arithmetic  9.74 us (2%)
    pallas_call x2, Pallas kernels, gather_blocks(): pl.pallas_call(functools.partial(gather_kernel, groups, mps), out_shape=j...  185 us
    dot_general x6, matrix products, matmul_t(): lax.dot_general(a, b, (((1,), (1,)), ((), ())), preferred_element_type=f32)  64.6 us
    dot_general x7, matrix products, matmul(): return jnp.dot(a, b, preferred_element_type=f32)  49.5 us
    all_to_all x1, blocking collectives, local(): lax.all_to_all(partial.reshape(group_rows, mps, share).swapaxes(0, 1), 'm...  29.3 us
    all_gather x1, waiting for transfers between devices, local(): placed = lax.all_gather(placed, 'mp', axis=1, tiled=True)  26.3 us
  transfers between devices with their start and end apart: 15, of which 4 were waited for; matrix products, arithmetic and copies ran while one was open for 21% of the time, Pallas kernels for 39%

profile of v3, /device:TPU:0, one launch (start us, length us, event | category | flops | bytes accessed | tf_op | source)
XLA Modules:
  0.0 470.9 jit_solution(12370363603652504121)
XLA Ops:
  7.2 0.7 all-gather.7.cloned.1.call-update
  7.9 2.5 copy.63
  10.4 8.5 %all-to-all-start = ((bf16[256,16,128]{0,2,1:T(8,128)(2,1)}), bf16[256,16,128]{0,2,1:T(8,128)(2,1)}, u32[]{:S(2)}, u32[]{:S(2)}) async-start(bf16[256,16,128]{0,2,1:T(8,128)(2,1)} %bitcast.79), calls=%async_computation | async-start | bytes 2097152 | tf_op jit(solution)/shard_map/all_to_all | solution.py:226
  19.0 0.7 all-gather.9.cloned.1.call-update
  19.7 1.4 convert_reduce_fusion
  21.1 2.5 psum.14
  23.6 1.5 fusion.12
  25.1 2.5 psum.15
  27.6 2.4 fusion.15.x_ref
  30.0 143.4 %shard_map.166 = bf16[4,4,64,6400]{3,2,1,0:T(8,128)(2,1)} custom-call(bf16[64,6400]{1,0:T(8,128)(2,1)} %fusion.15.x_ref), custom_call_target="tpu_custom_call" | custom-call | bytes 26214400 | tf_op jit(solution)/shard_map/pallas_call | solution.py:172
  173.5 2.3 copy.64
  175.9 5.5 %fusion = f32[512,256]{1,0:T(8,128)} fusion(bf16[6400,256]{1,0:T(8,128)(2,1)S(1)} %copy-done, bf16[1024,6400]{1,0:T(8,128)(2,1)} %bitcast.75, s32[]{:T(128)S(6)} %select_n.116), kind=kOutput, calls=%fused_computation.2 | convolution fusion | flops 1677721600 | bytes 10354692 | tf_op jit(solution)/shard_map/dot_general | solution.py:244
  181.9 0.8 dynamic-slice_bitcast_fusion
  182.6 2.0 all-gather
  184.6 6.5 %fusion.26.x_ref = bf16[512,256]{1,0:T(8,128)(2,1)} fusion(f32[512,256]{1,0:T(8,128)} %collective-permute-done, bf16[6400,256]{1,0:T(8,128)(2,1)S(1)} %copy-done, bf16[1024,6400]{1,0:T(8,128)(2,1)} %bitcast.76, s32[]{:T(128)S(6)} %select_n.115, f32[256]{0:T(256)S(1)} %copy-done.11), kind=kOutput, calls=%fused_computation.37 | convolution fusion | flops 1686503424 | bytes 10617860 | tf_op jit(solution)/shard_map/dot_general | solution.py:244
  191.1 41.2 %shard_map.167 = bf16[4,4,512,256]{3,2,1,0:T(8,128)(2,1)} custom-call(bf16[512,256]{1,0:T(8,128)(2,1)} %fusion.26.x_ref), custom_call_target="tpu_custom_call" | custom-call | bytes 8388608 | tf_op jit(solution)/shard_map/pallas_call | solution.py:172
  232.3 7.3 %copy.62 = bf16[512,4,4,256]{0,3,2,1:T(8,128)(2,1)} copy(bf16[512,4,4,256]{3,0,1,2:T(8,128)(2,1)} %bitcast.74) | data formatting | bytes 8388608 | tf_op jit(solution)/shard_map/transpose | solution.py:260
  239.7 4.2 fusion.22
  244.0 3.9 all_to_all.113
  247.9 3.2 gather_fusion
  251.4 8.7 %all_to_all.114 = bf16[4,256,128]{2,1,0:T(8,128)(2,1)S(1)} all-to-all(bf16[4,256,128]{2,1,0:T(8,128)(2,1)S(1)} %broadcast_select_fusion.1), channel_id=1, replica_groups=mesh['group'=4,'dp'=2,'mp'=4] {'group'}, dimensions={0} | all-to-all | bytes 524288 | tf_op jit(solution)/shard_map/all_to_all | solution.py:270
  260.1 0.7 copy_bitcast_fusion.2
  261.2 26.3 %all-gather.13.cloned.1.call-done = bf16[256,2048]{1,0:T(8,128)(2,1)} async-done(((bf16[256,512]{1,0:T(8,128)(2,1)}), bf16[256,2048]{1,0:T(8,128)(2,1)}) %all-gather.13.cloned.1.call-update) | async-done | bytes 1048592 | tf_op jit(solution)/shard_map/all_gather | solution.py:271
  287.5 1.4 broadcast_select_fusion
  288.9 8.6 %fusion.39 = f32[128,3584]{1,0:T(8,128)} fusion(bf16[2048,3584]{1,0:T(8,128)(2,1)} %param.24, bf16[256,2048]{1,0:T(8,128)(2,1)S(1)} %broadcast_select_fusion, s32[]{:T(128)S(6)} %select_n.120), kind=kOutput, calls=%fused_computation.58 | convolution fusion | flops 1879048192 | bytes 17039364 | tf_op jit(solution)/shard_map/dot_general | solution.py:244
  297.5 11.3 %fusion.27 = f32[128,3584]{1,0:T(8,128)} fusion(bf16[3584,2048]{1,0:T(8,128)(2,1)} %param.26, bf16[256,2048]{1,0:T(8,128)(2,1)S(1)} %copy-done.5, s32[]{:T(128)S(6)} %select_n.120), kind=kOutput, calls=%fused_computation.40 | convolution fusion | flops 1879048192 | bytes 17039364 | tf_op jit(solution)/shard_map/dot_general | solution.py:247
  309.4 7.2 %fusion.41 = f32[128,3584]{1,0:T(8,128)S(1)} fusion(bf16[2048,3584]{1,0:T(8,128)(2,1)} %param.25, bf16[256,2048]{1,0:T(8,128)(2,1)S(1)} %broadcast_select_fusion, s32[]{:T(128)S(6)} %select_n.120), kind=kOutput, calls=%fused_computation.60 | convolution fusion | flops 1879048192 | bytes 17039364 | tf_op jit(solution)/shard_map/dot_general | solution.py:244
  316.7 8.5 %convolution_add_fusion = f32[128,3584]{1,0:T(8,128)} fusion(f32[128,3584]{1,0:T(8,128)S(1)} %collective-permute-done.3, bf16[2048,3584]{1,0:T(8,128)(2,1)} %param.24, bf16[256,2048]{1,0:T(8,128)(2,1)S(1)} %broadcast_select_fusion, s32[]{:T(128)S(6)} %select_n.119), kind=kOutput, calls=%fused_computation.6 | convolution fusion | flops 1879506944 | bytes 18874372 | tf_op jit(solution)/shard_map/dot_general | solution.py:244
  325.3 13.3 %multiply_convert_fusion = (bf16[128,3584]{1,0:T(8,128)(2,1)}, f32[128,3584]{1,0:T(8,128)}) fusion(f32[128,3584]{1,0:T(8,128)} %convolution_add_fusion, f32[128,3584]{1,0:T(8,128)} %collective-permute-done.1, bf16[3584,2048]{1,0:T(8,128)(2,1)} %param.26, bf16[256,2048]{1,0:T(8,128)(2,1)} %all-gather.9.cloned.1.call-done, s32[]{:T(128)S(6)} %select_n.119), kind=kOutput, calls=%fused_computation.21 | convolution fusion | flops 1882259456 | bytes 21626884 | tf_op jit(solution)/shard_map/dot_general | solution.py:247
  338.5 8.9 %fusion.7 = bf16[128,3584]{1,0:T(8,128)(2,1)S(1)} fusion(f32[128,3584]{1,0:T(8,128)} %get-tuple-element.13, f32[128,3584]{1,0:T(8,128)} %collective-permute-done.2, bf16[2048,3584]{1,0:T(8,128)(2,1)} %param.25, f32[128,3584]{1,0:T(8,128)S(1)} %copy-done.2, bf16[256,2048]{1,0:T(8,128)(2,1)S(1)} %broadcast_select_fusion, s32[]{:T(128)S(6)} %select_n.119), kind=kOutput, calls=%fused_computation.12 | convolution fusion | flops 1884094464 | bytes 21626884 | tf_op jit(solution)/shard_map/dot_general | solution.py:244
  347.5 10.0 %fusion.62 = f32[128,2048]{1,0:T(8,128)S(1)} fusion(bf16[128,3584]{1,0:T(8,128)(2,1)S(1)} %fusion.7, bf16[2048,3584]{1,0:T(8,128)(2,1)} %param.24), kind=kOutput, calls=%fused_computation.106 | convolution fusion | flops 1879048192 | bytes 16646144 | tf_op jit(solution)/shard_map/dot_general | solution.py:247
  358.1 9.9 %fusion.8 = bf16[128,2048]{1,0:T(8,128)(2,1)S(1)} fusion(f32[128,2048]{1,0:T(8,128)S(1)} %fusion.62, bf16[128,3584]{1,0:T(8,128)(2,1)S(1)} %copy-done.4, bf16[2048,3584]{1,0:T(8,128)(2,1)} %param.25), kind=kOutput, calls=%fused_computation.15 | convolution fusion | flops 1879572480 | bytes 17170432 | tf_op jit(solution)/shard_map/dot_general | solution.py:247
  368.1 9.9 %fusion.63 = f32[128,2048]{1,0:T(8,128)S(1)} fusion(bf16[128,3584]{1,0:T(8,128)(2,1)S(1)} %collective-permute-done.5, bf16[2048,3584]{1,0:T(8,128)(2,1)} %param.25), kind=kOutput, calls=%fused_computation.107 | convolution fusion | flops 1879048192 | bytes 16646144 | tf_op jit(solution)/shard_map/dot_general | solution.py:247
  378.0 10.2 %fusion.9 = bf16[128,2048]{1,0:T(8,128)(2,1)S(1)} fusion(f32[128,2048]{1,0:T(8,128)S(1)} %fusion.63, bf16[128,3584]{1,0:T(8,128)(2,1)S(1)} %collective-permute-done.4, bf16[2048,3584]{1,0:T(8,128)(2,1)} %param.24), kind=kOutput, calls=%fused_computation.16 | convolution fusion | flops 1879572480 | bytes 17170432 | tf_op jit(solution)/shard_map/dot_general | solution.py:247
  388.6 29.3 %all_to_all.115 = bf16[4,256,512]{2,1,0:T(8,128)(2,1)S(1)} all-to-all(bf16[4,256,512]{2,1,0:T(8,128)(2,1)S(1)} %fusion.23), channel_id=1, replica_groups=mesh['group'=4,'dp'=2,'mp'=4] {'mp'}, dimensions={0} | all-to-all | bytes 2097152 | tf_op jit(solution)/shard_map/all_to_all | solution.py:298
  418.0 0.9 reduce_sum.61
  418.9 0.7 copy.66
  419.6 4.7 all-to-all-start.2
  424.5 9.4 %all-to-all-done.2 = bf16[16,64,128]{2,1,0:T(8,128)(2,1)} async-done(((bf16[16,64,128]{2,1,0:T(8,128)(2,1)}), bf16[16,64,128]{2,1,0:T(8,128)(2,1)}, u32[]{:S(2)}, u32[]{:S(2)}) %all-to-all-start.2) | async-done | bytes 262176 | tf_op jit(solution)/shard_map/all_to_all | solution.py:276
  433.9 4.0 all-to-all-start.5
  438.1 8.1 %all-gather.15.cloned.1.call-done = bf16[1024,512]{1,0:T(8,128)(2,1)} async-done(((bf16[256,512]{1,0:T(8,128)(2,1)}), bf16[1024,512]{1,0:T(8,128)(2,1)}) %all-gather.15.cloned.1.call-update) | async-done | bytes 1048592 | tf_op jit(solution)/shard_map/all_gather | solution.py:303
  446.2 2.6 gather_fusion.1
  448.8 0.8 select_select_fusion
  449.7 4.6 all-to-all-start.6
  454.3 1.7 copy_bitcast_fusion.3
  455.9 1.7 copy.80
  457.6 5.6 %all-to-all-done.6 = bf16[4,64,512]{2,1,0:T(8,128)(2,1)S(1)} async-done(((bf16[4,64,512]{2,1,0:T(8,128)(2,1)}), bf16[4,64,512]{2,1,0:T(8,128)(2,1)S(1)}, u32[]{:S(2)}, u32[]{:S(2)}) %all-to-all-start.6) | async-done | bytes 262176 | tf_op jit(solution)/shard_map/all_to_all | solution.py:313
  463.2 0.7 copy.81
  (76 shorter events, 3.6 us)
Async XLA Ops:
  7.2 168.7 %copy-start = (bf16[6400,256]{1,0:T(8,128)(2,1)S(1)}, bf16[6400,256]{1,0:T(8,128)(2,1)}, u32[]{:S(2)}) copy-start(bf16[6400,256]{1,0:T(8,128)(2,1)} %param.18) | copy-start | bytes 9830404
  7.2 184.0 %all-gather.7.cloned.1.call-start = ((), (), s32[]{:S(2)}) async-start(), calls=%async_computation.7 | async-start | bytes 1310720 | tf_op jit(solution)/shard_map/all_gather | solution.py:232
  10.4 17.2 %copy-start.6 = (f32[6400]{0:T(1024)S(1)}, f32[6400]{0:T(1024)}, u32[]{:S(2)}) copy-start(f32[6400]{0:T(1024)} %param.17) | copy-start | bytes 76804
  10.4 17.2 %copy-start.7 = (f32[6400]{0:T(1024)S(1)}, f32[6400]{0:T(1024)}, u32[]{:S(2)}) copy-start(f32[6400]{0:T(1024)} %param.16) | copy-start | bytes 76804
  10.4 163.1 %all-to-all-start = ((bf16[256,16,128]{0,2,1:T(8,128)(2,1)}), bf16[256,16,128]{0,2,1:T(8,128)(2,1)}, u32[]{:S(2)}, u32[]{:S(2)}) async-start(bf16[256,16,128]{0,2,1:T(8,128)(2,1)} %bitcast.79), calls=%async_computation | async-start | bytes 2097152 | tf_op jit(solution)/shard_map/all_to_all | solution.py:226
  18.9 172.2 %all-gather.9.cloned.1.call-start = ((), (), s32[]{:S(2)}) async-start(), calls=%async_computation.8 | async-start | bytes 1310720 | tf_op jit(solution)/shard_map/all_gather | solution.py:233
  19.7 220.0 %all-gather.11.cloned.1.call-start = ((), (), s32[]{:S(2)}) async-start(), calls=%async_computation.9 | async-start | bytes 3145728 | tf_op jit(solution)/shard_map/all_gather | solution.py:227
  175.8 111.7 %all-gather.13.cloned.1.call-start = ((), (), s32[]{:S(2)}) async-start(), calls=%async_computation.10 | async-start | bytes 1310720 | tf_op jit(solution)/shard_map/all_gather | solution.py:271
  175.9 5.6 %copy-start.10 = (s32[16]{0:T(128)S(1)}, s32[16]{0:T(128)}, u32[]{:S(2)}) copy-start(s32[16]{0:T(128)} %param.27) | copy-start | bytes 196
  175.9 5.8 %copy-start.8 = (s32[16]{0:T(128)S(1)}, s32[16]{0:T(128)}, u32[]{:S(2)}) copy-start(s32[16]{0:T(128)} %param.29) | copy-start | bytes 196
  175.9 5.8 %copy-start.9 = (s32[16]{0:T(128)S(1)}, s32[16]{0:T(128)}, u32[]{:S(2)}) copy-start(s32[16]{0:T(128)} %param.28) | copy-start | bytes 196
  175.9 8.7 %copy-start.11 = (f32[256]{0:T(256)S(1)}, f32[256]{0:T(256)}, u32[]{:S(2)}) copy-start(f32[256]{0:T(256)} %param.19) | copy-start | bytes 3076
  181.4 3.2 collective-permute-start
  247.9 39.6 %copy-start.3 = (bf16[256,2048]{1,0:T(8,128)(2,1)S(1)}, bf16[256,2048]{1,0:T(8,128)(2,1)}, u32[]{:S(2)}) copy-start(bf16[256,2048]{1,0:T(8,128)(2,1)} %all-gather.7.cloned.1.call-done) | copy-start | bytes 3145732
  260.8 185.4 %all-gather.15.cloned.1.call-start = ((), (), s32[]{:S(2)}) async-start(), calls=%async_computation.11 | async-start | bytes 1310720 | tf_op jit(solution)/shard_map/all_gather | solution.py:303
  288.9 8.6 %copy-start.5 = (bf16[256,2048]{1,0:T(8,128)(2,1)S(1)}, bf16[256,2048]{1,0:T(8,128)(2,1)}, u32[]{:S(2)}) copy-start(bf16[256,2048]{1,0:T(8,128)(2,1)} %all-gather.9.cloned.1.call-done) | copy-start | bytes 3145732
  297.5 19.2 %collective-permute-start.3 = (f32[128,3584]{1,0:T(8,128)}, f32[128,3584]{1,0:T(8,128)S(1)}, u32[]{:S(2)}, u32[]{:S(2)}) collective-permute-start(f32[128,3584]{1,0:T(8,128)} %fusion.39), channel_id=1, source_target_pairs={{0,4},{4,0},{1,5},{5,1},{2,6},{6,2},{3,7},{7,3},{8,12},{12,8},{9,1... | collective-permute-start | bytes 5505032 | tf_op jit(solution)/shard_map/ppermute | solution.py:190
  308.9 16.4 %collective-permute-start.1 = (f32[128,3584]{1,0:T(8,128)}, f32[128,3584]{1,0:T(8,128)}, u32[]{:S(2)}, u32[]{:S(2)}) collective-permute-start(f32[128,3584]{1,0:T(8,128)} %fusion.27), channel_id=1, source_target_pairs={{0,4},{4,0},{1,5},{5,1},{2,6},{6,2},{3,7},{7,3},{8,12},{12,8},{9,1... | collective-permute-start | bytes 5505032 | tf_op jit(solution)/shard_map/ppermute | solution.py:190
  316.6 21.9 %collective-permute-start.2 = (f32[128,3584]{1,0:T(8,128)S(1)}, f32[128,3584]{1,0:T(8,128)}, u32[]{:S(2)}, u32[]{:S(2)}) collective-permute-start(f32[128,3584]{1,0:T(8,128)S(1)} %fusion.41), channel_id=1, source_target_pairs={{0,4},{4,0},{1,5},{5,1},{2,6},{6,2},{3,7},{7,3},{8,12},{12,8},{9,1... | collective-permute-start | bytes 5505032 | tf_op jit(solution)/shard_map/ppermute | solution.py:190
  325.3 13.3 %copy-start.2 = (f32[128,3584]{1,0:T(8,128)S(1)}, f32[128,3584]{1,0:T(8,128)}, u32[]{:S(2)}) copy-start(f32[128,3584]{1,0:T(8,128)} %convolution_add_fusion) | copy-start | bytes 5505028
  347.4 10.5 %copy-start.4 = (bf16[128,3584]{1,0:T(8,128)(2,1)S(1)}, bf16[128,3584]{1,0:T(8,128)(2,1)}, u32[]{:S(2)}) copy-start(bf16[128,3584]{1,0:T(8,128)(2,1)} %get-tuple-element.12) | copy-start | bytes 2752516
  357.4 20.5 %collective-permute-start.4 = (bf16[128,3584]{1,0:T(8,128)(2,1)S(1)}, bf16[128,3584]{1,0:T(8,128)(2,1)S(1)}, u32[]{:S(2)}, u32[]{:S(2)}) collective-permute-start(bf16[128,3584]{1,0:T(8,128)(2,1)S(1)} %fusion.7), channel_id=1, source_target_pairs={{0,4},{4,0},{1,5},{5,1},{2,6},{6,2},{3,7},{7,3},{8,12},{12,8},{9,1... | collective-permute-start | bytes 2752520 | tf_op jit(solution)/shard_map/ppermute | solution.py:190
  358.0 10.1 %collective-permute-start.5 = (bf16[128,3584]{1,0:T(8,128)(2,1)S(1)}, bf16[128,3584]{1,0:T(8,128)(2,1)S(1)}, u32[]{:S(2)}, u32[]{:S(2)}) collective-permute-start(bf16[128,3584]{1,0:T(8,128)(2,1)S(1)} %copy-done.4), channel_id=1, source_target_pairs={{0,4},{4,0},{1,5},{5,1},{2,6},{6,2},{3,7},{7,3},{8,12},{12,8},{9,1... | collective-permute-start | bytes 2752520 | tf_op jit(solution)/shard_map/ppermute | solution.py:190
  419.6 14.3 %all-to-all-start.2 = ((bf16[16,64,128]{2,1,0:T(8,128)(2,1)}), bf16[16,64,128]{2,1,0:T(8,128)(2,1)}, u32[]{:S(2)}, u32[]{:S(2)}) async-start(bf16[16,64,128]{2,1,0:T(8,128)(2,1)} %bitcast.12), calls=%async_computation.2 | async-start | bytes 524288 | tf_op jit(solution)/shard_map/all_to_all | solution.py:276
  433.9 15.8 %all-to-all-start.5 = ((bf16[4,64,512]{2,1,0:T(8,128)(2,1)}), bf16[4,64,512]{2,1,0:T(8,128)(2,1)}, u32[]{:S(2)}, u32[]{:S(2)}) async-start(bf16[4,64,512]{2,1,0:T(8,128)(2,1)} %bitcast.80), calls=%async_computation.5 | async-start | bytes 524288 | tf_op jit(solution)/shard_map/all_to_all | solution.py:314
  438.1 25.8 %copy-start.1 = (bf16[6400,256]{1,0:T(8,128)(2,1)S(1)}, bf16[6400,256]{1,0:T(8,128)(2,1)}, u32[]{:S(2)}) copy-start(bf16[6400,256]{1,0:T(8,128)(2,1)} %param.18) | copy-start | bytes 9830404
  449.7 13.5 %all-to-all-start.6 = ((bf16[4,64,512]{2,1,0:T(8,128)(2,1)}), bf16[4,64,512]{2,1,0:T(8,128)(2,1)S(1)}, u32[]{:S(2)}, u32[]{:S(2)}) async-start(bf16[4,64,512]{2,1,0:T(8,128)(2,1)} %select_select_fusion), calls=%async_computation.6 | async-start | bytes 524288 | tf_op jit(solution)/shard_map/all_to_all | solution.py:313
Sparse Core Ops, SparseCore 0:
  9.6 50.3 all-gather.6
  61.6 38.7 all-gather.8
  175.9 9.3 all-gather.10
  260.9 26.5 all-gather.12
  419.0 27.1 all-gather.14
